TPU v7x, 32 devices: a whole 2x2x4 slice. The times are simulated.
32 devices in a mesh: segment: 4 (over y, core), dp: 8 (over z, x).
Axes of the slice: x: 2, y: 2, z: 4, core: 2. Of those that a mesh axis runs over, the one named last changes fastest.
Arguments:
- inputs: bfloat16 [2, 512, 4096], P(None, 'dp'), may hold values from -6 to 6
- cotangent: bfloat16 [2, 512, 4096], P(None, 'dp'), may hold values from -2 to 2
- w_in: bfloat16 [4, 2, 64, 64, 256], P('segment', None, 'dp'), may hold values from -0.75 to 0.75
- w_out: bfloat16 [4, 2, 64, 64, 256], P('segment', None, 'dp'), may hold values from -0.375 to 0.375
- gains: bfloat16 [4, 2, 4096], P('segment', None, 'dp'), may hold values from 0.25 to 1.75
- counts: int32 [4], replicated, may hold values from 1 to 2, 6 in all
Outputs:
- segment_out: bfloat16 [4, 2, 512, 4096], P('segment', None, 'dp')
- segment_grad: bfloat16 [4, 2, 512, 4096], P('segment', None, 'dp')
- grad_in: float32 [4, 2, 64, 64, 256], P('segment', None, 'dp')
- grad_out: float32 [4, 2, 64, 64, 256], P('segment', None, 'dp')
- grad_gain: float32 [4, 2, 4096], P('segment', None, 'dp')
All inputs are finite; a program needn't handle non-finite values.
Results may differ from a plain program's by a relative error of at most 0.023.
Values may be sent and summed in bfloat16 or wider, within the bound.
A program may use at most 192 MiB of HBM per device.

v0:
```python
from functools import partial

import jax
import jax.numpy as jnp
from jax import lax
from jax.sharding import PartitionSpec as P


def from_behind(block, axis, distance):
    devices = range(lax.axis_size(axis))
    route = [(i - distance, i) for i in devices if i - distance in devices]
    return lax.ppermute(block, axis, route)


def as_sent(value):
    return jax.tree.map(lambda a: a.astype(jnp.bfloat16) if a.dtype == jnp.float32 else a, value)


def layer(stream, weight_in, weight_out, gain_row):
    row_count = stream.shape[0]
    block_count = weight_in.shape[0]
    block_out = weight_in.shape[2]
    widened = stream.astype(jnp.float32)
    mean_square = jnp.mean(widened * widened, axis=-1, keepdims=True)
    normed = (widened * lax.rsqrt(mean_square + 1e-05) * gain_row).astype(jnp.bfloat16)
    blocks = normed.reshape(row_count, block_count, weight_in.shape[1])
    hidden = jnp.einsum("tbi,bio->tbo", blocks, weight_in, preferred_element_type=jnp.float32)
    permuted = jnp.transpose(hidden, (0, 2, 1)).reshape(row_count, block_count, block_out)
    active = jax.nn.gelu(permuted, approximate=True).astype(jnp.bfloat16)
    update = jnp.einsum("tbo,bio->tbi", active, weight_out, preferred_element_type=jnp.float32)
    return (widened + update.reshape(row_count, -1)).astype(jnp.bfloat16)


def per_device(inputs, cotangent, w_in, w_out, gains, counts):
    segment_count = lax.axis_size("segment")
    my_segment = lax.axis_index("segment")
    slot_count = w_in.shape[1]
    micro_count = inputs.shape[0]
    tick_count = micro_count + segment_count - 1
    count_here = jnp.sum(jnp.where(jnp.arange(segment_count) == my_segment, counts, 0))
    full_in, full_out, full_gain = (
        lax.all_gather(w_in, "dp", axis=2, tiled=True),
        lax.all_gather(w_out, "dp", axis=2, tiled=True),
        lax.all_gather(gains, "dp", axis=2, tiled=True),
    )

    def run_slot(stream_in, slot_number):
        return layer(
            stream_in, full_in[0, slot_number], full_out[0, slot_number], full_gain[0, slot_number]
        )

    def keep_stream(stream_in):
        return stream_in

    def section(stream_in):
        slot_inputs = []
        for slot_number in range(slot_count):
            slot_inputs.append(stream_in)
            stream_in = lax.cond(
                slot_number < count_here,
                partial(run_slot, slot_number=slot_number),
                keep_stream,
                stream_in,
            )
        return (stream_in, jnp.stack(slot_inputs))

    def section_spare(stream_in):
        return (stream_in, jnp.broadcast_to(stream_in, (slot_count,) + stream_in.shape))

    stream_shape = inputs.shape[1:]
    outputs_init = jnp.zeros(inputs.shape, jnp.bfloat16)
    stored_init = jnp.zeros(inputs.shape, jnp.bfloat16)

    def forward_tick(step_index, carried):
        incoming, outputs, stored = carried
        micro_index = step_index - my_segment
        is_live = (micro_index >= 0) & (micro_index < micro_count)
        position = jnp.clip(micro_index, 0, micro_count - 1)
        first_input = lax.dynamic_index_in_dim(
            inputs, jnp.clip(step_index, 0, micro_count - 1), 0, keepdims=False
        )
        entry = jnp.where(my_segment == 0, first_input, incoming)
        result, slot_inputs = lax.cond(is_live, section, section_spare, entry)
        old_output = lax.dynamic_index_in_dim(outputs, position, 0, keepdims=False)
        outputs = lax.dynamic_update_index_in_dim(
            outputs, jnp.where(is_live, result, old_output), position, 0
        )
        old_kept = lax.dynamic_index_in_dim(stored, position, 0, keepdims=False)
        stored = lax.dynamic_update_index_in_dim(
            stored, jnp.where(is_live, entry, old_kept), position, 0
        )
        return (result, outputs, stored)

    def forward_step(step_index, carried):
        result, outputs, stored = forward_tick(step_index, carried)
        passed = from_behind(result, "segment", 1)
        return (passed, outputs, stored)

    carried = lax.fori_loop(
        0,
        tick_count - 1,
        forward_step,
        (jnp.zeros(stream_shape, jnp.bfloat16), outputs_init, stored_init),
    )
    unused_result, outputs, stored = forward_tick(tick_count - 1, carried)

    def slot_backward(slot_number, stream_in, upstream):

        def pulled(operands):
            value, grad_here = operands
            unused_out, pullback = jax.vjp(
                layer,
                value,
                full_in[0, slot_number],
                full_out[0, slot_number],
                full_gain[0, slot_number],
            )
            return pullback(grad_here)

        def skipped(operands):
            value, grad_here = operands
            return (
                grad_here,
                jnp.zeros(full_in.shape[2:], jnp.bfloat16),
                jnp.zeros(full_out.shape[2:], jnp.bfloat16),
                jnp.zeros(full_gain.shape[2:], jnp.bfloat16),
            )

        return lax.cond(slot_number < count_here, pulled, skipped, (stream_in, upstream))

    def section_back(operands):
        kept_value, upstream, buffer_in, buffer_out, buffer_gain, position = operands
        unused_stream, slot_inputs = section(kept_value)
        first_list = [None] * slot_count
        second_list = [None] * slot_count
        gain_list = [None] * slot_count
        for slot_number in reversed(range(slot_count)):
            upstream, first_list[slot_number], second_list[slot_number], gain_list[slot_number] = (
                slot_backward(slot_number, slot_inputs[slot_number], upstream)
            )
        buffer_in = lax.dynamic_update_index_in_dim(buffer_in, jnp.stack(first_list), position, 0)
        buffer_out = lax.dynamic_update_index_in_dim(
            buffer_out, jnp.stack(second_list), position, 0
        )
        buffer_gain = lax.dynamic_update_index_in_dim(
            buffer_gain, jnp.stack(gain_list), position, 0
        )
        return (upstream, buffer_in, buffer_out, buffer_gain)

    def section_back_spare(operands):
        kept_value, upstream, buffer_in, buffer_out, buffer_gain, position = operands
        return (upstream, buffer_in, buffer_out, buffer_gain)

    def backward_tick(step_index, carried):
        incoming, grads_kept, buffer_in, buffer_out, buffer_gain = carried
        micro_index = step_index - (segment_count - 1 - my_segment)
        is_live = (micro_index >= 0) & (micro_index < micro_count)
        position = jnp.clip(micro_index, 0, micro_count - 1)
        last_grad = lax.dynamic_index_in_dim(
            cotangent, jnp.clip(step_index, 0, micro_count - 1), 0, keepdims=False
        )
        entry_grad = jnp.where(my_segment == segment_count - 1, last_grad, incoming)
        kept_value = lax.dynamic_index_in_dim(stored, position, 0, keepdims=False)
        down, buffer_in, buffer_out, buffer_gain = lax.cond(
            is_live,
            section_back,
            section_back_spare,
            (kept_value, entry_grad, buffer_in, buffer_out, buffer_gain, position),
        )
        old_grad = lax.dynamic_index_in_dim(grads_kept, position, 0, keepdims=False)
        grads_kept = lax.dynamic_update_index_in_dim(
            grads_kept, jnp.where(is_live, down, old_grad), position, 0
        )
        return (down, grads_kept, buffer_in, buffer_out, buffer_gain)

    def backward_step(step_index, carried):
        down, grads_kept, buffer_in, buffer_out, buffer_gain = backward_tick(step_index, carried)
        passed = from_behind(as_sent(down), "segment", -1).astype(down.dtype)
        return (passed, grads_kept, buffer_in, buffer_out, buffer_gain)

    back_init = (
        jnp.zeros(stream_shape, jnp.bfloat16),
        jnp.zeros(inputs.shape, jnp.bfloat16),
        jnp.zeros((micro_count,) + full_in.shape[1:], jnp.bfloat16),
        jnp.zeros((micro_count,) + full_out.shape[1:], jnp.bfloat16),
        jnp.zeros((micro_count,) + full_gain.shape[1:], jnp.bfloat16),
    )
    carried = lax.fori_loop(0, tick_count - 1, backward_step, back_init)
    unused_down, grads_kept, buffer_in, buffer_out, buffer_gain = backward_tick(
        tick_count - 1, carried
    )
    total_in = jnp.sum(buffer_in.astype(jnp.float32), axis=0)
    total_out = jnp.sum(buffer_out.astype(jnp.float32), axis=0)
    total_gain = jnp.sum(buffer_gain.astype(jnp.float32), axis=0)
    summed_in, summed_out, summed_gain = (
        lax.psum_scatter(
            total_in[None].astype(jnp.bfloat16), "dp", scatter_dimension=2, tiled=True
        ).astype(jnp.float32),
        lax.psum_scatter(
            total_out[None].astype(jnp.bfloat16), "dp", scatter_dimension=2, tiled=True
        ).astype(jnp.float32),
        lax.psum_scatter(
            total_gain[None].astype(jnp.bfloat16), "dp", scatter_dimension=2, tiled=True
        ).astype(jnp.float32),
    )
    return (outputs[None], grads_kept[None], summed_in, summed_out, summed_gain)


def solution(mesh):
    in_specs = (
        P(None, "dp", None),
        P(None, "dp", None),
        P("segment", None, "dp", None, None),
        P("segment", None, "dp", None, None),
        P("segment", None, "dp"),
        P(),
    )
    out_specs = (
        P("segment", None, "dp", None),
        P("segment", None, "dp", None),
        P("segment", None, "dp", None, None),
        P("segment", None, "dp", None, None),
        P("segment", None, "dp"),
    )
    return jax.shard_map(
        per_device, mesh=mesh, in_specs=in_specs, out_specs=out_specs, check_vma=False
    )
```

profile of v0, /device:TPU:8, one launch (start us, length us, event | category | flops | bytes accessed | tf_op | source)
XLA Modules:
  0.0 1378.4 jit_solution(18338499100445268482)
XLA Ops:
  8.7 25.4 %all_gather.9 = bf16[1,2,4096]{2,1,0:T(2,128)(2,1)S(1)} all-gather(bf16[1,2,512]{2,1,0:T(2,128)(2,1)} %param.42), channel_id=1, replica_groups=mesh['segment'=4,'dp'=8] {'dp'}, dimensions={2}, use_global_device_ids=true | all-gather | bytes 18432 | tf_op jit(solution)/shard_map/all_gather | solution.py:44
  35.3 48.9 %all-gather.3.cloned.1.call-done = bf16[1,2,64,64,256]{4,3,2,1,0:T(8,128)(2,1)} async-done(((bf16[1,2,8,64,256]{4,3,2,1,0:T(8,128)(2,1)}), bf16[1,2,64,64,256]{4,3,2,1,0:T(8,128)(2,1)}) %all-gather.3.cloned.1.call-update) | async-done | bytes 4194320 | tf_op jit(solution)/shard_map/all_gather | solution.py:42
  84.3 73.9 %all-gather.5.cloned.1.call-done = bf16[1,2,64,64,256]{4,3,2,1,0:T(8,128)(2,1)} async-done(((bf16[1,2,8,64,256]{4,3,2,1,0:T(8,128)(2,1)}), bf16[1,2,64,64,256]{4,3,2,1,0:T(8,128)(2,1)}) %all-gather.5.cloned.1.call-update) | async-done | bytes 4194320 | tf_op jit(solution)/shard_map/all_gather | solution.py:43
  160.3 185.6 %while.41 = (s32[]{:T(128)}, bf16[64,4096]{1,0:T(8,128)(2,1)S(1)}, bf16[2,64,4096]{2,1,0:T(8,128)(2,1)}, bf16[2,64,4096]{2,1,0:T(8,128)(2,1)}, s32[]{:T(128)}, /...) while((s32[]{:T(128)}, bf16[64,4096]{1,0:T(8,128)(2,1)S(1)}, ...), condition=%wide.region_10.11_spmd, body=%wide.region_1.10_spmd.sunk | while | flops 561782912 | bytes 130108384 | solution.py:99
  163.5 61.6 %conditional.18 = (bf16[64,4096]{1,0:T(8,128)(2,1)S(1)}) conditional(s32[]{:T(128)} %convert_element_type.813, bf16[64,4096]{1,0:T(8,128)(2,1)S(1)} %get-tuple-element.1244, (s32[]{:T(128)}, bf16[64,4096]{1,0:T(8,128)(2,1)S(1)}, bf16[1,2,4096]{2,1,0:T(2,128)(2,1)S(1)}, bf16[1,2,64,64,256]{4,3,2,1,0:T(8,128)(2,1)}, ...), branch_computations={%region_2.2_spmd, %region_3.9_spmd} | conditional | flops 560996480 | bytes 121718944 | solution.py:83
  164.0 30.2 %conditional = (bf16[64,4096]{1,0:T(8,128)(2,1)S(1)}) conditional(s32[]{:T(128)} %convert_element_type.392, bf16[64,4096]{1,0:T(8,128)(2,1)S(1)} %get-tuple-element.846, (bf16[64,4096]{1,0:T(8,128)(2,1)S(1)}, bf16[1,2,4096]{2,1,0:T(2,128)(2,1)S(1)}, bf16[1,2,64,64,256]{4,3,2,1,0:T(8,128)(2,1)}, bf16[1,2,64,64,256]{4,3,2,1,0:T(8,128)(2,1)}) %tuple.159), branch_computations={%region_4.3_spmd, %region_5.5_spmd} | conditional | flops 280498240 | bytes 60859428 | solution.py:59
  194.8 30.2 %conditional.1 = (bf16[64,4096]{1,0:T(8,128)(2,1)S(1)}) conditional(s32[]{:T(128)} %convert_element_type.391, bf16[64,4096]{1,0:T(8,128)(2,1)S(1)} %get-tuple-element.1405, (bf16[64,4096]{1,0:T(8,128)(2,1)S(1)}, bf16[1,2,4096]{2,1,0:T(2,128)(2,1)S(1)}, bf16[1,2,64,64,256]{4,3,2,1,0:T(8,128)(2,1)}, bf16[1,2,64,64,256]{4,3,2,1,0:T(8,128)(2,1)}) %tuple.160), branch_computations={%region_7.6_spmd, %region_8.8_spmd} | conditional | flops 280498240 | bytes 60859428 | solution.py:59
  231.5 61.6 %conditional.18 = (bf16[64,4096]{1,0:T(8,128)(2,1)S(1)}) conditional(s32[]{:T(128)} %convert_element_type.813, bf16[64,4096]{1,0:T(8,128)(2,1)S(1)} %get-tuple-element.1244, (s32[]{:T(128)}, bf16[64,4096]{1,0:T(8,128)(2,1)S(1)}, bf16[1,2,4096]{2,1,0:T(2,128)(2,1)S(1)}, bf16[1,2,64,64,256]{4,3,2,1,0:T(8,128)(2,1)}, ...), branch_computations={%region_2.2_spmd, %region_3.9_spmd} | conditional | flops 560996480 | bytes 121718944 | solution.py:83
  232.1 30.2 %conditional = (bf16[64,4096]{1,0:T(8,128)(2,1)S(1)}) conditional(s32[]{:T(128)} %convert_element_type.392, bf16[64,4096]{1,0:T(8,128)(2,1)S(1)} %get-tuple-element.846, (bf16[64,4096]{1,0:T(8,128)(2,1)S(1)}, bf16[1,2,4096]{2,1,0:T(2,128)(2,1)S(1)}, bf16[1,2,64,64,256]{4,3,2,1,0:T(8,128)(2,1)}, bf16[1,2,64,64,256]{4,3,2,1,0:T(8,128)(2,1)}) %tuple.159), branch_computations={%region_4.3_spmd, %region_5.5_spmd} | conditional | flops 280498240 | bytes 60859428 | solution.py:59
  262.9 30.2 %conditional.1 = (bf16[64,4096]{1,0:T(8,128)(2,1)S(1)}) conditional(s32[]{:T(128)} %convert_element_type.391, bf16[64,4096]{1,0:T(8,128)(2,1)S(1)} %get-tuple-element.1405, (bf16[64,4096]{1,0:T(8,128)(2,1)S(1)}, bf16[1,2,4096]{2,1,0:T(2,128)(2,1)S(1)}, bf16[1,2,64,64,256]{4,3,2,1,0:T(8,128)(2,1)}, bf16[1,2,64,64,256]{4,3,2,1,0:T(8,128)(2,1)}) %tuple.160), branch_computations={%region_7.6_spmd, %region_8.8_spmd} | conditional | flops 280498240 | bytes 60859428 | solution.py:59
  299.6 33.1 %collective-permute-start = (bf16[64,4096]{1,0:T(8,128)(2,1)S(1)}, bf16[64,4096]{1,0:T(8,128)(2,1)S(1)}, u32[]{:S(2)}, u32[]{:S(2)}) collective-permute-start(bf16[64,4096]{1,0:T(8,128)(2,1)S(1)} %get-tuple-element.1413), channel_id=1, source_target_pairs={{0,8},{8,16},{16,24},{1,9},{9,17},{17,25},{2,10},{10,18},{18,26},{... | collective-permute-start | bytes 1572872 | tf_op jit(solution)/shard_map/while/body/eval_jaxpr/ppermute | solution.py:12
  359.0 606.4 %while.42 = (s32[]{:T(128)}, bf16[64,4096]{1,0:T(8,128)(2,1)S(1)}, bf16[2,64,4096]{2,1,0:T(8,128)(2,1)}, bf16[2,2,64,64,256]{4,3,2,1,0:T(8,128)(2,1)}, bf16[2,2,...) while((s32[]{:T(128)}, bf16[64,4096]{1,0:T(8,128)(2,1)S(1)}, ...), condition=%wide.region_35.36_spmd, body=%wide.region_19.35_spmd.sunk | while | flops 1719702272 | bytes 293896256 | solution.py:188
  367.9 7.8 conditional.19
  378.9 37.9 %collective-permute-done.1 = bf16[64,4096]{1,0:T(8,128)(2,1)S(1)} collective-permute-done((bf16[64,4096]{1,0:T(8,128)(2,1)S(1)}, bf16[64,4096]{1,0:T(8,128)(2,1)S(1)}, u32[]{:S(2)}, u32[]{:S(2)}) %collective-permute-start.1) | collective-permute-done | bytes 524320 | tf_op jit(solution)/shard_map/while/body/eval_jaxpr/ppermute | solution.py:12
  433.2 360.3 %collective-permute-done.1 = bf16[64,4096]{1,0:T(8,128)(2,1)S(1)} collective-permute-done((bf16[64,4096]{1,0:T(8,128)(2,1)S(1)}, bf16[64,4096]{1,0:T(8,128)(2,1)S(1)}, u32[]{:S(2)}, u32[]{:S(2)}) %collective-permute-start.1) | collective-permute-done | bytes 524320 | tf_op jit(solution)/shard_map/while/body/eval_jaxpr/ppermute | solution.py:12
  794.6 154.6 %conditional.19 = ((bf16[64,4096]{1,0:T(8,128)(2,1)S(1)}, bf16[2,2,64,64,256]{4,3,2,1,0:T(8,128)(2,1)}, bf16[2,2,64,64,256]{4,3,2,1,0:T(8,128)(2,1)}, bf16[2,2,4096]{2,1,0:T(2,128)(2,1)S(1)})) conditional(s32[]{:T(128)} %convert_element_type.814, (bf16[64,4096]{1,0:T(8,128)(2,1)S(1)}, bf16[2,2,64,64,256]{4,3,2,1,0:T(8,128)(2,1)}, ...), branch_computations={%region_20.20_spmd, %region_21.34_spmd} | conditional | flops 1719177984 | bytes 287603904 | solution.py:164
  796.3 30.3 %conditional.5 = (bf16[64,4096]{1,0:T(8,128)(2,1)S(1)}) conditional(s32[]{:T(128)} %convert_element_type.452, bf16[64,4096]{1,0:T(8,128)(2,1)S(1)} %dynamic-slice_bitcast_fusion, (bf16[64,4096]{1,0:T(8,128)(2,1)S(1)}, bf16[1,2,4096]{2,1,0:T(2,128)(2,1)S(1)}, bf16[1,2,64,64,256]{4,3,2,1,0:T(8,128)(2,1)}, ...), branch_computations={%region_22.21_spmd, %region_23.23_spmd} | conditional | flops 280498240 | bytes 60859428 | solution.py:59
  827.2 55.9 %conditional.6 = (bf16[64,4096]{1,0:T(8,128)(2,1)S(1)}, bf16[1,64,64,256]{3,2,1,0:T(8,128)(2,1)}, bf16[1,64,64,256]{3,2,1,0:T(8,128)(2,1)S(1)}, bf16[1,4096]{1,0:T(2,128)(2,1)S(1)}) conditional(s32[]{:T(128)} %convert_element_type.453, bf16[64,4096]{1,0:T(8,128)(2,1)S(1)} %get-tuple-element.890, (bf16[64,4096]{1,0:T(8,128)(2,1)S(1)}, ...), branch_computations={%region_25.24_spmd, %region_26.28_spmd} | conditional | flops 710934912 | bytes 101288920 | solution.py:129
  839.9 7.6 reshape.358
  884.4 58.5 %conditional.7 = (bf16[64,4096]{1,0:T(8,128)(2,1)S(1)}, bf16[1,64,64,256]{3,2,1,0:T(8,128)(2,1)}, bf16[1,64,64,256]{3,2,1,0:T(8,128)(2,1)}, bf16[1,4096]{1,0:T(2,128)(2,1)S(1)}) conditional(s32[]{:T(128)} %convert_element_type.452, bf16[64,4096]{1,0:T(8,128)(2,1)S(1)} %get-tuple-element.896, (bf16[64,4096]{1,0:T(8,128)(2,1)S(1)}, ...), branch_computations={%region_30.29_spmd, %region_31.33_spmd} | conditional | flops 710934912 | bytes 99191736 | solution.py:129
  898.9 7.6 reshape.362
  966.4 154.8 %conditional.15 = ((bf16[64,4096]{1,0:T(8,128)(2,1)S(1)}, bf16[2,2,64,64,256]{4,3,2,1,0:T(8,128)(2,1)}, bf16[2,2,64,64,256]{4,3,2,1,0:T(8,128)(2,1)}, bf16[2,2,4096]{2,1,0:T(2,128)(2,1)S(1)})) conditional(s32[]{:T(128)} %convert_element_type.510, (bf16[64,4096]{1,0:T(8,128)(2,1)S(1)}, bf16[2,2,64,64,256]{4,3,2,1,0:T(8,128)(2,1)}, ...), branch_computations={%region_36.37_spmd, %region_37.51_spmd} | conditional | flops 1719177984 | bytes 287603904 | solution.py:164
  968.1 30.3 %conditional.9 = (bf16[64,4096]{1,0:T(8,128)(2,1)S(1)}) conditional(s32[]{:T(128)} %convert_element_type.499, bf16[64,4096]{1,0:T(8,128)(2,1)S(1)} %dynamic-slice_bitcast_fusion.1, (bf16[64,4096]{1,0:T(8,128)(2,1)S(1)}, bf16[1,2,4096]{2,1,0:T(2,128)(2,1)S(1)}, bf16[1,2,64,64,256]{4,3,2,1,0:T(8,128)(2,1)}, ...), branch_computations={%region_38.38_spmd, %region_39.40_spmd} | conditional | flops 280498240 | bytes 60859428 | solution.py:59
  999.0 56.0 %conditional.10 = (bf16[64,4096]{1,0:T(8,128)(2,1)S(1)}, bf16[1,64,64,256]{3,2,1,0:T(8,128)(2,1)}, bf16[1,64,64,256]{3,2,1,0:T(8,128)(2,1)S(1)}, bf16[1,4096]{1,0:T(2,128)(2,1)S(1)}) conditional(s32[]{:T(128)} %convert_element_type.500, bf16[64,4096]{1,0:T(8,128)(2,1)S(1)} %get-tuple-element.941, (bf16[64,4096]{1,0:T(8,128)(2,1)S(1)}, ...), branch_computations={%region_41.41_spmd, %region_42.45_spmd} | conditional | flops 710934912 | bytes 101288920 | solution.py:129
  1011.9 7.6 reshape.369
  1056.3 58.5 %conditional.11 = (bf16[64,4096]{1,0:T(8,128)(2,1)S(1)}, bf16[1,64,64,256]{3,2,1,0:T(8,128)(2,1)}, bf16[1,64,64,256]{3,2,1,0:T(8,128)(2,1)}, bf16[1,4096]{1,0:T(2,128)(2,1)S(1)}) conditional(s32[]{:T(128)} %convert_element_type.499, bf16[64,4096]{1,0:T(8,128)(2,1)S(1)} %get-tuple-element.947, (bf16[64,4096]{1,0:T(8,128)(2,1)S(1)}, ...), branch_computations={%region_46.46_spmd, %region_47.50_spmd} | conditional | flops 710934912 | bytes 99191736 | solution.py:129
  1070.8 7.6 reshape.373
  1125.2 8.6 reduce_sum.240
  1141.4 8.7 reduce_sum.241
  1163.2 23.4 %reduce-scatter.16.cloned.1.call-done = bf16[512,2]{1,0:T(8,128)(2,1)} async-done(((bf16[4096,2]{1,0:T(8,128)(2,1)}), bf16[512,2]{1,0:T(8,128)(2,1)}) %reduce-scatter.16.cloned.1.call-update) | async-done | bytes 2064
  1188.4 89.5 %reduce-scatter.12.cloned.1.call-done = bf16[8,32768]{1,0:T(8,128)(2,1)} async-done(((bf16[64,32768]{1,0:T(8,128)(2,1)}), bf16[8,32768]{1,0:T(8,128)(2,1)}) %reduce-scatter.12.cloned.1.call-update) | async-done | bytes 524304
  1279.0 90.0 %reduce-scatter.14.cloned.1.call-done = bf16[8,32768]{1,0:T(8,128)(2,1)} async-done(((bf16[64,32768]{1,0:T(8,128)(2,1)}), bf16[8,32768]{1,0:T(8,128)(2,1)}) %reduce-scatter.14.cloned.1.call-update) | async-done | bytes 524304
  (318 shorter events, 504.2 us)
Async XLA Ops:
  7.2 77.1 %all-gather.3.cloned.1.call-start = ((), (), s32[]{:S(2)}) async-start(), calls=%async_computation.3 | async-start | bytes 4718592 | tf_op jit(solution)/shard_map/all_gather | solution.py:42
  7.9 150.2 %all-gather.5.cloned.1.call-start = ((), (), s32[]{:S(2)}) async-start(), calls=%async_computation.4 | async-start | bytes 4718592 | tf_op jit(solution)/shard_map/all_gather | solution.py:43
  8.6 1177.9 %reduce-scatter.16.cloned.1.call-start = ((), (), s32[]{:S(2)}) async-start(), calls=%async_computation.7 | async-start | bytes 1179648
  185.0 3.6 copy-start
  225.1 3.3 collective-permute-start
  293.1 3.3 collective-permute-start
  299.6 35.2 %collective-permute-start = (bf16[64,4096]{1,0:T(8,128)(2,1)S(1)}, bf16[64,4096]{1,0:T(8,128)(2,1)S(1)}, u32[]{:S(2)}, u32[]{:S(2)}) collective-permute-start(bf16[64,4096]{1,0:T(8,128)(2,1)S(1)} %get-tuple-element.1413), channel_id=1, source_target_pairs={{0,8},{8,16},{16,24},{1,9},{9,17},{17,25},{2,10},{10,18},{18,26},{... | collective-permute-start | bytes 1572872 | tf_op jit(solution)/shard_map/while/body/eval_jaxpr/ppermute | solution.py:12
  337.9 8.0 collective-permute-start
  375.6 41.2 %collective-permute-start.1 = (bf16[64,4096]{1,0:T(8,128)(2,1)S(1)}, bf16[64,4096]{1,0:T(8,128)(2,1)S(1)}, u32[]{:S(2)}, u32[]{:S(2)}) collective-permute-start(bf16[64,4096]{1,0:T(8,128)(2,1)S(1)} %get-tuple-element.1260), channel_id=1, source_target_pairs={{8,0},{16,8},{24,16},{9,1},{17,9},{25,17},{10,2},{18,10},{26,18},{... | collective-permute-start | bytes 1572872 | tf_op jit(solution)/shard_map/while/body/eval_jaxpr/ppermute | solution.py:12
  418.1 10.5 collective-permute-start.1
  429.9 363.6 %collective-permute-start.1 = (bf16[64,4096]{1,0:T(8,128)(2,1)S(1)}, bf16[64,4096]{1,0:T(8,128)(2,1)S(1)}, u32[]{:S(2)}, u32[]{:S(2)}) collective-permute-start(bf16[64,4096]{1,0:T(8,128)(2,1)S(1)} %get-tuple-element.1260), channel_id=1, source_target_pairs={{8,0},{16,8},{24,16},{9,1},{17,9},{25,17},{10,2},{18,10},{26,18},{... | collective-permute-start | bytes 1572872 | tf_op jit(solution)/shard_map/while/body/eval_jaxpr/ppermute | solution.py:12
  827.2 5.7 copy-start.6
  828.1 11.8 copy-start.7
  873.3 4.0 copy-start.8
  875.2 4.1 copy-start.12
  875.2 4.1 copy-start.16
  887.1 11.8 copy-start.9
  932.0 3.7 copy-start.10
  933.8 4.0 copy-start.13
  933.8 4.0 copy-start.18
  949.3 8.3 collective-permute-start.1
  999.0 5.7 copy-start.21
  999.9 12.0 copy-start.22
  1045.2 4.0 copy-start.23
  1047.1 4.1 copy-start.27
  1047.1 4.1 copy-start.30
  1059.1 11.8 copy-start.24
  1104.0 3.7 copy-start.25
  1105.7 4.0 copy-start.28
  1105.7 4.0 copy-start.32
  1125.1 152.7 %reduce-scatter.12.cloned.1.call-start = ((), (), s32[]{:S(2)}) async-start(), calls=%async_computation.5 | async-start | bytes 4718592
  1140.9 228.1 %reduce-scatter.14.cloned.1.call-start = ((), (), s32[]{:S(2)}) async-start(), calls=%async_computation.6 | async-start | bytes 4718592
  (14 other events, 31.3 us)
Sparse Core Ops, SparseCore 0:
  10.2 74.0 all-gather.2
  86.4 71.6 all-gather.4
  1125.3 61.2 reduce-scatter.15
  1190.5 87.2 reduce-scatter.11
  1281.3 87.6 reduce-scatter.13
where the time goes:
time: 1400 us; the launch traced here: 1380 us
  waiting for transfers between devices  737 us (53%)
  local copies, waits for them, and re-layouts  294 us (21%)
  matrix products  120 us (9%)
  other arithmetic  108 us (8%)
  starting transfers between devices  47.7 us (3%)
  loops' own time  32.3 us (2%)
  blocking collectives  25.4 us (2%)
  between operations  14.1 us (1%)
    ppermute x8, waiting for transfers between devices, from_behind(): return lax.ppermute(block, axis, route)  410 us
    unnamed x8, waiting for transfers between devices  204 us
    reshape x14, local copies, waits for them, and re-layouts, layer(): jnp.transpose(hidden, (0, 2, 1)).reshape(row_count, block_count, block_out)  88.6 us
    all_gather x1, waiting for transfers between devices, per_device(): lax.all_gather(w_out, 'dp', axis=2, tiled=True)  73.9 us
    transpose x10, local copies, waits for them, and re-layouts, layer(): jnp.transpose(hidden, (0, 2, 1)).reshape(row_count, block_count, block_out)  69.8 us
    dot_general x18, matrix products, layer(): jnp.einsum('tbi,bio->tbo', blocks, weight_in, preferred_element_type=jnp....  65.9 us
    dot_general x14, matrix products, layer(): jnp.einsum('tbo,bio->tbi', active, weight_out, preferred_element_type=jnp...  53.6 us
    all_gather x1, waiting for transfers between devices, per_device(): lax.all_gather(w_in, 'dp', axis=2, tiled=True)  48.9 us
  transfers between devices with their start and end apart: 13, of which 9 were waited for; matrix products, arithmetic and copies ran while one was open for 4% of the time, Pallas kernels for 0%

commit v1 on v0

v1 whole, which is shorter than its diff:
```python
from functools import partial

import jax
import jax.numpy as jnp
from jax import lax
from jax.experimental import pallas as pl
from jax.experimental.pallas import tpu as pltpu
from jax.sharding import PartitionSpec as P

EPS = 1e-05
GROUP = 8
VMEM_BYTES = 48 * 1024 * 1024
C0 = 0.7978845608028654
C1 = 0.044715


def dot_tn(a, b):
    return lax.dot_general(a, b, (((0,), (0,)), ((), ())), preferred_element_type=jnp.float32)


def dot_nt(a, b):
    return lax.dot_general(a, b, (((1,), (1,)), ((), ())), preferred_element_type=jnp.float32)


def dot_nn(a, b):
    return lax.dot_general(a, b, (((1,), (0,)), ((), ())), preferred_element_type=jnp.float32)


def inverse_rms(x_ref, chunk):
    width, tokens = x_ref.shape

    def add(i, total):
        x = x_ref[pl.ds(pl.multiple_of(i * chunk, chunk), chunk), :].astype(jnp.float32)
        return total + jnp.sum((x * x).reshape(chunk // 8, 8, tokens), axis=0)

    total = lax.fori_loop(0, width // chunk, add, jnp.zeros((8, tokens), jnp.float32), unroll=4)
    mean = jnp.sum(total, axis=0, keepdims=True) / width
    return lax.rsqrt(mean + EPS)


def forward_kernel(x_ref, w_in_ref, w_out_ref, gain_ref, y_ref, act_ref, slope_ref, hid_ref, r_ref):
    step = pl.program_id(0)
    steps = pl.num_programs(0) // 2
    group, bi, bo = w_in_ref.shape
    nb = group * steps

    @pl.when(step == 0)
    def _():
        r_ref[...] = jnp.broadcast_to(inverse_rms(x_ref, bi), r_ref.shape)

    @pl.when(step < steps)
    def _():
        r = r_ref[0:1, :]
        for k in range(group):
            b = step * group + k
            rows = pl.ds(pl.multiple_of(b * bi, bi), bi)
            x = x_ref[rows, :].astype(jnp.float32)
            normed = (x * r * gain_ref[rows, :].astype(jnp.float32)).astype(jnp.bfloat16)
            hid_ref[pl.ds(b, bo, stride=nb), :] = dot_tn(w_in_ref[k], normed)

    @pl.when(step >= steps)
    def _():
        for k in range(group):
            b = (step - steps) * group + k
            rows = pl.ds(pl.multiple_of(b * bi, bi), bi)
            h = hid_ref[pl.ds(pl.multiple_of(b * bo, bo), bo), :]
            sq = h * h
            th = jnp.tanh(C0 * h * (1.0 + C1 * sq))
            half = 0.5 * (1.0 + th)
            act = (h * half).astype(jnp.bfloat16)
            slope = half + 0.5 * h * (1.0 - th * th) * (C0 * (1.0 + 3.0 * C1 * sq))
            own = pl.ds(k * bo, bo)
            act_ref[own, :] = act
            slope_ref[own, :] = slope.astype(jnp.bfloat16)
            v = dot_nn(w_out_ref[k], act)
            y_ref[rows, :] = (x_ref[rows, :].astype(jnp.float32) + v).astype(jnp.bfloat16)


def backward_kernel(
    x_ref, g_ref, w_in_ref, w_out_ref, gain_ref, act_ref, slope_ref,
    dx_ref, d_in_ref, d_out_ref, d_gain_ref, hid_ref, q_ref, r_ref, s_ref,
):
    step = pl.program_id(0)
    steps = pl.num_programs(0) // 2
    group, bi, bo = w_in_ref.shape
    nb = group * steps

    @pl.when(step == 0)
    def _():
        r_ref[...] = jnp.broadcast_to(inverse_rms(x_ref, bi), r_ref.shape)
        s_ref[...] = jnp.zeros_like(s_ref)

    @pl.when(step < steps)
    def _():
        for k in range(group):
            b = step * group + k
            g = g_ref[pl.ds(pl.multiple_of(b * bi, bi), bi), :]
            own = pl.ds(k * bo, bo)
            d_act = dot_tn(w_out_ref[k], g)
            hid_ref[pl.ds(pl.multiple_of(b * bo, bo), bo), :] = d_act * slope_ref[own, :].astype(
                jnp.float32
            )
            d_out_ref[k] = dot_nt(g, act_ref[own, :]).astype(jnp.bfloat16)

    @pl.when(step >= steps)
    def _():
        r = r_ref[0:1, :]
        for k in range(group):
            b = (step - steps) * group + k
            rows = pl.ds(pl.multiple_of(b * bi, bi), bi)
            d_hid = hid_ref[pl.ds(b, bo, stride=nb), :].astype(jnp.bfloat16)
            d_norm = dot_nn(w_in_ref[k], d_hid)
            x = x_ref[rows, :].astype(jnp.float32)
            gain = gain_ref[rows, :].astype(jnp.float32)
            unit = x * r
            normed = (unit * gain).astype(jnp.bfloat16)
            d_in_ref[k] = dot_nt(normed, d_hid).astype(jnp.bfloat16)
            d_gain_ref[rows, :] = jnp.sum(d_norm * unit, axis=1, keepdims=True)
            q = d_norm * gain
            q_ref[rows, :] = q
            s_ref[...] += jnp.sum((q * x).reshape(bi // 8, 8, q.shape[1]), axis=0)

    @pl.when(step == 2 * steps - 1)
    def _():
        width = x_ref.shape[0]
        r = r_ref[0:1, :]
        s = jnp.sum(s_ref[...], axis=0, keepdims=True) * (r * r * r) / width

        def finish(i, carry):
            rows = pl.ds(pl.multiple_of(i * bi, bi), bi)
            x = x_ref[rows, :].astype(jnp.float32)
            g = g_ref[rows, :].astype(jnp.float32)
            dx_ref[rows, :] = (g + (q_ref[rows, :] * r - x * s)).astype(jnp.bfloat16)
            return carry

        lax.fori_loop(0, width // bi, finish, 0, unroll=4)


def whole(shape):
    return pl.BlockSpec(shape, lambda i: (0,) * len(shape))


def forward_layer(x, w_in, w_out, gain):
    width, tokens = x.shape
    nb, bi, bo = w_in.shape
    group = min(GROUP, nb)
    steps = nb // group
    first = lambda i: (jnp.minimum(i, steps - 1), 0, 0)
    second = lambda i: (jnp.maximum(i - steps, 0), 0, 0)
    second2 = lambda i: (jnp.maximum(i - steps, 0), 0)
    return pl.pallas_call(
        forward_kernel,
        grid=(2 * steps,),
        out_shape=(
            jax.ShapeDtypeStruct((width, tokens), jnp.bfloat16),
            jax.ShapeDtypeStruct((nb * bo, tokens), jnp.bfloat16),
            jax.ShapeDtypeStruct((nb * bo, tokens), jnp.bfloat16),
        ),
        in_specs=[
            whole((width, tokens)),
            pl.BlockSpec((group, bi, bo), first),
            pl.BlockSpec((group, bi, bo), second),
            whole((width, tokens)),
        ],
        out_specs=(
            whole((width, tokens)),
            pl.BlockSpec((group * bo, tokens), second2),
            pl.BlockSpec((group * bo, tokens), second2),
        ),
        scratch_shapes=[
            pltpu.VMEM((nb * bo, tokens), jnp.float32),
            pltpu.VMEM((8, tokens), jnp.float32),
        ],
        compiler_params=pltpu.CompilerParams(vmem_limit_bytes=VMEM_BYTES),
        name="layer_forward",
    )(x, w_in, w_out, gain)


def backward_layer(x, g, w_in, w_out, gain, act, slope):
    width, tokens = x.shape
    nb, bi, bo = w_in.shape
    group = min(GROUP, nb)
    steps = nb // group
    first = lambda i: (jnp.minimum(i, steps - 1), 0, 0)
    first2 = lambda i: (jnp.minimum(i, steps - 1), 0)
    second = lambda i: (jnp.maximum(i - steps, 0), 0, 0)
    weight = jax.ShapeDtypeStruct((nb, bi, bo), jnp.bfloat16)
    return pl.pallas_call(
        backward_kernel,
        grid=(2 * steps,),
        out_shape=(
            jax.ShapeDtypeStruct((width, tokens), jnp.bfloat16),
            weight,
            weight,
            jax.ShapeDtypeStruct((width, 1), jnp.float32),
        ),
        in_specs=[
            whole((width, tokens)),
            whole((width, tokens)),
            pl.BlockSpec((group, bi, bo), second),
            pl.BlockSpec((group, bi, bo), first),
            whole((width, tokens)),
            pl.BlockSpec((group * bo, tokens), first2),
            pl.BlockSpec((group * bo, tokens), first2),
        ],
        out_specs=(
            whole((width, tokens)),
            pl.BlockSpec((group, bi, bo), second),
            pl.BlockSpec((group, bi, bo), first),
            whole((width, 1)),
        ),
        scratch_shapes=[
            pltpu.VMEM((nb * bo, tokens), jnp.float32),
            pltpu.VMEM((width, tokens), jnp.float32),
            pltpu.VMEM((8, tokens), jnp.float32),
            pltpu.VMEM((8, tokens), jnp.float32),
        ],
        compiler_params=pltpu.CompilerParams(vmem_limit_bytes=VMEM_BYTES),
        name="layer_backward",
    )(x, g, w_in, w_out, gain, act, slope)


def to_columns(a):
    micro, rows, width = a.shape
    return a.reshape(micro * rows, width).T


def per_device(inputs, cotangent, w_in, w_out, gains, counts):
    segment_count = lax.axis_size("segment")
    my_segment = lax.axis_index("segment")
    slot_count = w_in.shape[1]
    micro, rows, width = inputs.shape
    tokens = micro * rows
    count_here = jnp.sum(jnp.where(jnp.arange(segment_count) == my_segment, counts, 0))
    full_in = [lax.all_gather(w_in[0, l], "dp", axis=0, tiled=True) for l in range(slot_count)]
    full_out = [lax.all_gather(w_out[0, l], "dp", axis=0, tiled=True) for l in range(slot_count)]
    full_gain = lax.all_gather(gains[0], "dp", axis=1, tiled=True)
    gain = [
        jnp.broadcast_to(full_gain[l][:, None], (width, tokens)) for l in range(slot_count)
    ]
    nb, bi, bo = full_in[0].shape
    first_x = to_columns(inputs)
    last_g = to_columns(cotangent)

    def run_forward(operands):
        x, saved = operands
        kept = []
        for l in range(slot_count):
            def live(x, l=l):
                return forward_layer(x, full_in[l], full_out[l], gain[l])

            if l == 0:
                y, act, slope = live(x)
            else:
                y, act, slope = lax.cond(
                    l < count_here, live, lambda x, l=l: (x, saved[l][1], saved[l][2]), x
                )
            kept.append((x, act, slope))
            x = y
        return x, tuple(kept)

    def keep(operands):
        return operands

    hid = jnp.zeros((nb * bo, tokens), jnp.bfloat16)
    saved = tuple((first_x, hid, hid) for l in range(slot_count))
    x = first_x
    result = x
    for k in range(segment_count):
        x, saved = lax.cond(my_segment == k, run_forward, keep, (x, saved))
        result = jnp.where(my_segment == k, x, result)
        if k < segment_count - 1:
            x = lax.ppermute(x, "segment", [(k, k + 1)])

    def run_backward(operands):
        g, grads = operands
        out = [None] * slot_count
        for l in reversed(range(slot_count)):
            x, act, slope = saved[l]

            def live(g, l=l, x=x, act=act, slope=slope):
                return backward_layer(x, g, full_in[l], full_out[l], gain[l], act, slope)

            if l == 0:
                g, *out[l] = live(g)
            else:
                g, *out[l] = lax.cond(l < count_here, live, lambda g, l=l: (g, *grads[l]), g)
        return g, tuple(tuple(o) for o in out)

    zero_weight = jnp.zeros((nb, bi, bo), jnp.bfloat16)
    zero_gain = jnp.zeros((width, 1), jnp.float32)
    grads = tuple((zero_weight, zero_weight, zero_gain) for l in range(slot_count))
    g = last_g
    down = g
    for k in reversed(range(segment_count)):
        g, grads = lax.cond(my_segment == k, run_backward, keep, (g, grads))
        down = jnp.where(my_segment == k, g, down)
        if k > 0:
            g = lax.ppermute(g, "segment", [(k, k - 1)])

    def scatter(a):
        return lax.psum_scatter(
            a.astype(jnp.bfloat16), "dp", scatter_dimension=0, tiled=True
        ).astype(jnp.float32)

    grad_in = jnp.stack([scatter(grads[l][0]) for l in range(slot_count)])[None]
    grad_out = jnp.stack([scatter(grads[l][1]) for l in range(slot_count)])[None]
    all_gain = jnp.stack([grads[l][2][:, 0] for l in range(slot_count)], axis=1)
    grad_gain = scatter(all_gain).T[None]
    outputs = result.T.reshape(1, micro, rows, width)
    grads_kept = down.T.reshape(1, micro, rows, width)
    return outputs, grads_kept, grad_in, grad_out, grad_gain


def solution(mesh):
    in_specs = (
        P(None, "dp", None),
        P(None, "dp", None),
        P("segment", None, "dp", None, None),
        P("segment", None, "dp", None, None),
        P("segment", None, "dp"),
        P(),
    )
    out_specs = (
        P("segment", None, "dp", None),
        P("segment", None, "dp", None),
        P("segment", None, "dp", None, None),
        P("segment", None, "dp", None, None),
        P("segment", None, "dp"),
    )
    return jax.shard_map(
        per_device, mesh=mesh, in_specs=in_specs, out_specs=out_specs, check_vma=False
    )
```

time: 1400 us -> 910 us (0.65)
  local copies, waits for them, and re-layouts: 294 us -> 51.5 us
  matrix products: 120 us -> 0 us
  other arithmetic: 108 us -> 12.2 us
  Pallas kernels: 0 us -> 39 us
  starting transfers between devices: 47.7 us -> 10.8 us
  loops' own time: 32.3 us -> 14.6 us
    reduce_scatter x0 -> x4, waiting for transfers between devices: none -> 278 us  [scatter(): lax.psum_scatter(a.astype(jnp.bfloat16), 'dp', scatter_dimension=0, tiled...]
    ppermute x8 -> x6, waiting for transfers between devices: 410 us -> 226 us  [the longest x3 225 us: per_device(): g = lax.ppermute(g, 'segment', [(k, k - 1)])]
    unnamed x8 -> x10, waiting for transfers between devices: 204 us -> 52.8 us
    dot_general x32 -> x0, matrix products: 120 us -> none  [the longest x18 65.9 us: layer(): jnp.einsum('tbi,bio->tbo', blocks, weight_in, preferred_element_type=jnp....]
    reshape x34 -> x0, local copies, waits for them, and re-layouts: 111 us -> none  [the longest x14 88.6 us: layer(): jnp.transpose(hidden, (0, 2, 1)).reshape(row_count, block_count, block_out)]
    transpose x20 -> x1, local copies, waits for them, and re-layouts: 96 us -> 2.27 us  [to_columns(): return a.reshape(micro * rows, width).T]
    all_gather x2 -> x4, waiting for transfers between devices: 123 us -> 174 us  [the longest x2 101 us: per_device(): lax.all_gather(w_out[0, l], 'dp', axis=0, tiled=True)]
    convert_element_type x38 -> x0, other arithmetic: 43.5 us -> none  [the longest x6 21.8 us: layer(): active = jax.nn.gelu(permuted, approximate=True).astype(jnp.bfloat16)]
  transfers between devices with their start and end apart: 13 -> 15, of which waited for: 9 -> 11; matrix products, arithmetic and copies ran while one was open for 4% -> 2% of each run, Pallas kernels for 0% -> 0%
where the time goes in v1:
time: 910 us; the launch traced here: 899 us
  waiting for transfers between devices  732 us (80%)
  local copies, waits for them, and re-layouts  51.5 us (6%)
  Pallas kernels  39 us (4%)
  blocking collectives  25.1 us (3%)
  loops' own time  14.6 us (2%)
  between operations  14.2 us (2%)
  other arithmetic  12.2 us (1%)
  starting transfers between devices  10.8 us (1%)
    reduce_scatter x4, waiting for transfers between devices, scatter(): lax.psum_scatter(a.astype(jnp.bfloat16), 'dp', scatter_dimension=0, tiled...  278 us
    ppermute x3, waiting for transfers between devices, per_device(): g = lax.ppermute(g, 'segment', [(k, k - 1)])  225 us
    all_gather x2, waiting for transfers between devices, per_device(): lax.all_gather(w_out[0, l], 'dp', axis=0, tiled=True)  101 us
    all_gather x2, waiting for transfers between devices, per_device(): lax.all_gather(w_in[0, l], 'dp', axis=0, tiled=True)  73.5 us
    unnamed x10, waiting for transfers between devices  52.8 us
    all_gather x1, blocking collectives, per_device(): full_gain = lax.all_gather(gains[0], 'dp', axis=1, tiled=True)  25.1 us
    pallas_call x1, Pallas kernels, backward_layer(): pl.pallas_call(backward_kernel, grid=(2 * steps,), out_shape=(jax.ShapeDt...  19.7 us
    pallas_call x1, Pallas kernels, forward_layer(): pl.pallas_call(forward_kernel, grid=(2 * steps,), out_shape=(jax.ShapeDty...  19.2 us
  transfers between devices with their start and end apart: 15, of which 11 were waited for; matrix products, arithmetic and copies ran while one was open for 2% of the time, Pallas kernels for 0%

profile of v1, /device:TPU:8, one launch (start us, length us, event | category | flops | bytes accessed | tf_op | source)
XLA Modules:
  0.0 899.2 jit_solution(6872733965139317419)
XLA Ops:
  12.5 25.1 %all-gather.2 = bf16[1,2,4096]{2,1,0:T(2,128)(2,1)S(1)} all-gather(bf16[1,2,512]{2,1,0:T(2,128)(2,1)S(1)} %copy-done.13), channel_id=4, replica_groups=mesh['segment'=4,'dp'=8] {'dp'}, dimensions={2}, use_global_device_ids=true | all-gather | bytes 18432 | tf_op jit(solution)/shard_map/all_gather | solution.py:237
  38.3 23.0 %all-gather.14.cloned.1.call-done = bf16[1,1,64,64,256]{4,3,1,0,2:T(8,128)(2,1)} async-done(((bf16[1,1,8,64,256]{4,3,1,0,2:T(8,128)(2,1)}), bf16[1,1,64,64,256]{4,3,1,0,2:T(8,128)(2,1)}) %all-gather.14.cloned.1.call-update) | async-done | bytes 2097168 | tf_op jit(solution)/shard_map/all_gather | solution.py:235
  61.3 50.5 %all-gather.10.cloned.1.call-done = bf16[1,1,64,64,256]{4,3,1,0,2:T(8,128)(2,1)} async-done(((bf16[1,1,8,64,256]{4,3,1,0,2:T(8,128)(2,1)}), bf16[1,1,64,64,256]{4,3,1,0,2:T(8,128)(2,1)}) %all-gather.10.cloned.1.call-update) | async-done | bytes 2097168 | tf_op jit(solution)/shard_map/all_gather | solution.py:235
  111.8 50.5 %all-gather.16.cloned.1.call-done = bf16[1,1,64,64,256]{4,3,1,0,2:T(8,128)(2,1)} async-done(((bf16[1,1,8,64,256]{4,3,1,0,2:T(8,128)(2,1)}), bf16[1,1,64,64,256]{4,3,1,0,2:T(8,128)(2,1)}) %all-gather.16.cloned.1.call-update) | async-done | bytes 2097168 | tf_op jit(solution)/shard_map/all_gather | solution.py:236
  162.3 50.4 %all-gather.12.cloned.1.call-done = bf16[1,1,64,64,256]{4,3,1,0,2:T(8,128)(2,1)} async-done(((bf16[1,1,8,64,256]{4,3,1,0,2:T(8,128)(2,1)}), bf16[1,1,64,64,256]{4,3,1,0,2:T(8,128)(2,1)}) %all-gather.12.cloned.1.call-update) | async-done | bytes 2097168 | tf_op jit(solution)/shard_map/all_gather | solution.py:236
  214.8 28.9 %conditional.16 = (bf16[4096,128]{1,0:T(8,128)(2,1)}, bf16[4096,128]{1,0:T(8,128)(2,1)}, bf16[16384,128]{1,0:T(8,128)(2,1)}, bf16[16384,128]{1,0:T(8,128)(2,1)},...) conditional(s32[]{:T(128)} %convert_element_type.49, ...), branch_computations={%region_1.2_spmd, %region_2.5_spmd} | conditional | flops 2 | bytes 23068736 | solution.py:270
  217.7 19.2 %layer_forward.9 = (bf16[4096,128]{1,0:T(8,128)(2,1)}, bf16[16384,128]{1,0:T(8,128)(2,1)}, bf16[16384,128]{1,0:T(8,128)(2,1)}) custom-call(bf16[4096,128]{1,0:T(8,128)(2,1)} %copy.51.x_ref, bf16[64,64,256]{2,1,0:T(8,128)(2,1)} %get-tuple-element.430.w_in_ref, bf16[64,64,256]{2,1,0:T(8,128)(2,1)} %get-tuple-element.431.w_out_ref, ...), custom_call_target="tpu_custom_call" | custom-call | tf_op jit(solution)/shard_map/cond/branch_1_fun/layer_forward/pallas_call | solution.py:151
  236.9 6.9 conditional
  241.4 2.4 broadcast_in_dim.38
  243.8 2.3 collective-permute-start
  247.7 2.3 conditional.17
  247.7 2.3 copy.73
  251.7 11.1 %conditional.18 = (bf16[4096,128]{1,0:T(8,128)(2,1)}, bf16[4096,128]{1,0:T(8,128)(2,1)}, bf16[16384,128]{1,0:T(8,128)(2,1)}, bf16[16384,128]{1,0:T(8,128)(2,1)},...) conditional(s32[]{:T(128)} %convert_element_type.47, ...), branch_computations={%region_9.10_spmd, %region_10.13_spmd} | conditional | flops 2 | bytes 14680258 | solution.py:270
  251.7 2.4 copy.75
  264.5 2.3 conditional.19
  264.5 2.3 copy.77
  266.8 11.6 %conditional.20 = (bf16[4096,128]{1,0:T(8,128)(2,1)}, bf16[64,64,256]{2,1,0:T(8,128)(2,1)}, bf16[64,64,256]{2,1,0:T(8,128)(2,1)}, f32[4096,1]{1,0:T(8,128)}, bf1...) conditional(s32[]{:T(128)} %convert_element_type.46, ...), branch_computations={%region_17.18_spmd, %region_18.21_spmd} | conditional | flops 2 | bytes 12583074 | solution.py:296
  280.1 2.3 conditional.21
  280.1 2.3 copy.80
  284.1 7.0 conditional.22
  292.4 224.7 %collective-permute-done.5 = bf16[4096,128]{1,0:T(8,128)(2,1)} collective-permute-done((bf16[4096,128]{1,0:T(8,128)(2,1)}, bf16[4096,128]{1,0:T(8,128)(2,1)}, u32[]{:S(2)}, u32[]{:S(2)}) %collective-permute-start.5) | collective-permute-done | bytes 1048608 | tf_op jit(solution)/shard_map/ppermute | solution.py:299
  517.2 24.9 %conditional.23 = (bf16[4096,128]{1,0:T(8,128)(2,1)}, bf16[64,64,256]{2,1,0:T(8,128)(2,1)}, bf16[64,64,256]{2,1,0:T(8,128)(2,1)}, bf16[64,64,256]{2,1,0:T(8,128)...) conditional(s32[]{:T(128)} %convert_element_type.49, ...), branch_computations={%region_29.30_spmd, %region_30.33_spmd} | conditional | flops 4098 | bytes 20996342 | solution.py:296
  517.7 2.7 conditional.7
  517.7 2.7 convert.22
  522.3 19.7 %layer_backward.15 = (bf16[4096,128]{1,0:T(8,128)(2,1)}, bf16[64,64,256]{2,1,0:T(8,128)(2,1)}, bf16[64,64,256]{2,1,0:T(8,128)(2,1)}, f32[4096,1]{1,0:T(8,128)}) custom-call(bf16[4096,128]{1,0:T(8,128)(2,1)} %get-tuple-element.602.x_ref, bf16[4096,128]{1,0:T(8,128)(2,1)S(1)} %copy.278.g_ref, bf16[64,64,256]{2,1,0:T(8,128)(2,1)S(1)} %copy-done.6, ...), custom_call_target="tpu_custom_call" | custom-call | tf_op jit(solution)/shard_map/cond/branch_1_fun/layer_backward/pallas_call | solution.py:188
  551.6 2.4 copy.61
  556.3 3.0 select_select_fusion
  559.3 48.9 %reduce-scatter.16.cloned.1.call-done = bf16[512,2]{1,0:T(8,128)(2,1)} async-done(((bf16[4096,2]{1,0:T(8,128)(2,1)}), bf16[512,2]{1,0:T(8,128)(2,1)}) %reduce-scatter.16.cloned.1.call-update) | async-done | bytes 2064
  609.8 68.3 %reduce-scatter.10.cloned.1.call-done = bf16[8,64,256]{2,1,0:T(8,128)(2,1)} async-done(((bf16[64,64,256]{2,1,0:T(8,128)(2,1)}), bf16[8,64,256]{2,1,0:T(8,128)(2,1)}) %reduce-scatter.10.cloned.1.call-update) | async-done | bytes 262160 | tf_op jit(solution)/shard_map/reduce_scatter | solution.py:302
  678.2 70.8 %reduce-scatter.8.cloned.1.call-done = bf16[8,64,256]{2,1,0:T(8,128)(2,1)} async-done(((bf16[64,64,256]{2,1,0:T(8,128)(2,1)}), bf16[8,64,256]{2,1,0:T(8,128)(2,1)}) %reduce-scatter.8.cloned.1.call-update) | async-done | bytes 262160 | tf_op jit(solution)/shard_map/reduce_scatter | solution.py:302
  751.0 68.6 %reduce-scatter.14.cloned.1.call-done = bf16[8,64,256]{2,1,0:T(8,128)(2,1)} async-done(((bf16[64,64,256]{2,1,0:T(8,128)(2,1)}), bf16[8,64,256]{2,1,0:T(8,128)(2,1)}) %reduce-scatter.14.cloned.1.call-update) | async-done | bytes 262160 | tf_op jit(solution)/shard_map/reduce_scatter | solution.py:302
  819.7 70.6 %reduce-scatter.12.cloned.1.call-done = bf16[8,64,256]{2,1,0:T(8,128)(2,1)} async-done(((bf16[64,64,256]{2,1,0:T(8,128)(2,1)}), bf16[8,64,256]{2,1,0:T(8,128)(2,1)}) %reduce-scatter.12.cloned.1.call-update) | async-done | bytes 262160 | tf_op jit(solution)/shard_map/reduce_scatter | solution.py:302
  (68 shorter events, 57.7 us)
Async XLA Ops:
  7.2 5.3 copy-start.13
  7.2 30.4 %copy-start.14 = (s32[4]{0:T(128)S(1)}, s32[4]{0:T(128)}, u32[]{:S(2)}) copy-start(s32[4]{0:T(128)} %param.43) | copy-start | bytes 52
  7.2 54.1 %all-gather.14.cloned.1.call-start = ((), (), s32[]{:S(2)}) async-start(), calls=%async_computation.11 | async-start | bytes 2359296 | tf_op jit(solution)/shard_map/all_gather | solution.py:235
  9.1 102.6 %all-gather.10.cloned.1.call-start = ((), (), s32[]{:S(2)}) async-start(), calls=%async_computation.9 | async-start | bytes 2359296 | tf_op jit(solution)/shard_map/all_gather | solution.py:235
  9.9 152.4 %all-gather.16.cloned.1.call-start = ((), (), s32[]{:S(2)}) async-start(), calls=%async_computation.12 | async-start | bytes 2359296 | tf_op jit(solution)/shard_map/all_gather | solution.py:236
  11.8 200.8 %all-gather.12.cloned.1.call-start = ((), (), s32[]{:S(2)}) async-start(), calls=%async_computation.10 | async-start | bytes 2359296 | tf_op jit(solution)/shard_map/all_gather | solution.py:236
  12.4 595.9 %reduce-scatter.16.cloned.1.call-start = ((), (), s32[]{:S(2)}) async-start(), calls=%async_computation.13 | async-start | bytes 1179648
  61.3 153.6 %copy-start = (bf16[1,1,64,64,256]{4,3,1,0,2:T(8,128)(2,1)S(1)}, bf16[1,1,64,64,256]{4,3,1,0,2:T(8,128)(2,1)}, u32[]{:S(2)}) copy-start(bf16[1,1,64,64,256]{4,3,1,0,2:T(8,128)(2,1)} %all-gather.14.cloned.1.call-done) | copy-start | bytes 6291460
  243.8 3.9 collective-permute-start
  250.0 1.7 collective-permute-start.1
  262.8 1.7 collective-permute-start.2
  278.4 1.7 collective-permute-start.3
  282.4 1.7 collective-permute-start.4
  291.1 226.0 %collective-permute-start.5 = (bf16[4096,128]{1,0:T(8,128)(2,1)}, bf16[4096,128]{1,0:T(8,128)(2,1)}, u32[]{:S(2)}, u32[]{:S(2)}) collective-permute-start(bf16[4096,128]{1,0:T(8,128)(2,1)} %get-tuple-element.730), channel_id=1, source_target_pairs={{8,0},{9,1},{10,2},{11,3},{12,4},{13,5},{14,6},{15,7}} | collective-permute-start | bytes 3145736 | tf_op jit(solution)/shard_map/ppermute | solution.py:299
  520.4 1.9 copy-start.6
  547.3 130.9 %reduce-scatter.10.cloned.1.call-start = ((), (), s32[]{:S(2)}) async-start(), calls=%async_computation.6 | async-start | bytes 2359296 | tf_op jit(solution)/shard_map/reduce_scatter | solution.py:302
  547.8 201.1 %reduce-scatter.8.cloned.1.call-start = ((), (), s32[]{:S(2)}) async-start(), calls=%async_computation.5 | async-start | bytes 2359296 | tf_op jit(solution)/shard_map/reduce_scatter | solution.py:302
  548.6 271.1 %reduce-scatter.14.cloned.1.call-start = ((), (), s32[]{:S(2)}) async-start(), calls=%async_computation.8 | async-start | bytes 2359296 | tf_op jit(solution)/shard_map/reduce_scatter | solution.py:302
  549.3 341.0 %reduce-scatter.12.cloned.1.call-start = ((), (), s32[]{:S(2)}) async-start(), calls=%async_computation.7 | async-start | bytes 2359296 | tf_op jit(solution)/shard_map/reduce_scatter | solution.py:302
  551.6 4.7 copy-start.11
  551.6 4.7 copy-start.12
Sparse Core Ops, SparseCore 0:
  10.7 50.4 all-gather.13
  64.0 47.7 all-gather.9
  114.5 47.7 all-gather.15
  164.8 47.7 all-gather.11
  547.4 60.8 reduce-scatter.15
  612.1 66.0 reduce-scatter.9
  682.1 66.7 reduce-scatter.7
  752.9 66.7 reduce-scatter.13
  823.6 66.6 reduce-scatter.11

commit v2 on v1

--- a/solution.py
+++ b/solution.py
@@ -41,7 +41,7 @@
 def forward_kernel(x_ref, w_in_ref, w_out_ref, gain_ref, y_ref, act_ref, slope_ref, hid_ref, r_ref):
     step = pl.program_id(0)
     steps = pl.num_programs(0) // 2
-    group, bi, bo = w_in_ref.shape
+    group, bi, bo = w_out_ref.shape
     nb = group * steps
 
     @pl.when(step == 0)
@@ -56,7 +56,7 @@
             rows = pl.ds(pl.multiple_of(b * bi, bi), bi)
             x = x_ref[rows, :].astype(jnp.float32)
             normed = (x * r * gain_ref[rows, :].astype(jnp.float32)).astype(jnp.bfloat16)
-            hid_ref[pl.ds(b, bo, stride=nb), :] = dot_tn(w_in_ref[k], normed)
+            hid_ref[pl.ds(b, bo, stride=nb), :] = dot_tn(w_in_ref[k, :bi, :], normed)
 
     @pl.when(step >= steps)
     def _():
@@ -78,11 +78,11 @@
 
 def backward_kernel(
     x_ref, g_ref, w_in_ref, w_out_ref, gain_ref, act_ref, slope_ref,
-    dx_ref, d_in_ref, d_out_ref, d_gain_ref, hid_ref, q_ref, r_ref, s_ref,
+    dx_ref, d_in_ref, d_out_ref, hid_ref, q_ref, r_ref, s_ref,
 ):
     step = pl.program_id(0)
     steps = pl.num_programs(0) // 2
-    group, bi, bo = w_in_ref.shape
+    group, bi, bo = w_out_ref.shape
     nb = group * steps
 
     @pl.when(step == 0)
@@ -109,13 +109,18 @@
             b = (step - steps) * group + k
             rows = pl.ds(pl.multiple_of(b * bi, bi), bi)
             d_hid = hid_ref[pl.ds(b, bo, stride=nb), :].astype(jnp.bfloat16)
-            d_norm = dot_nn(w_in_ref[k], d_hid)
+            d_norm = dot_nn(w_in_ref[k, :bi, :], d_hid)
             x = x_ref[rows, :].astype(jnp.float32)
             gain = gain_ref[rows, :].astype(jnp.float32)
             unit = x * r
             normed = (unit * gain).astype(jnp.bfloat16)
-            d_in_ref[k] = dot_nt(normed, d_hid).astype(jnp.bfloat16)
-            d_gain_ref[rows, :] = jnp.sum(d_norm * unit, axis=1, keepdims=True)
+            d_in_ref[k, :bi, :] = dot_nt(normed, d_hid).astype(jnp.bfloat16)
+            extra = d_in_ref.shape[1] - bi
+            ones = jnp.ones((extra, x.shape[1]), jnp.bfloat16)
+            d_gain = dot_nt(ones, (d_norm * unit).astype(jnp.bfloat16))
+            d_in_ref[k, bi:, :] = jnp.concatenate(
+                [d_gain, jnp.zeros((extra, bo - bi), jnp.float32)], axis=1
+            ).astype(jnp.bfloat16)
             q = d_norm * gain
             q_ref[rows, :] = q
             s_ref[...] += jnp.sum((q * x).reshape(bi // 8, 8, q.shape[1]), axis=0)
@@ -136,13 +141,366 @@
         lax.fori_loop(0, width // bi, finish, 0, unroll=4)
 
 
+MESH = pl.DeviceIdType.MESH
+
+
+def grid_of(dp):
+    x = 1
+    while 2 * (2 * x) * (2 * x) <= dp and dp % (2 * x) == 0:
+        x = 2 * x
+    return dp // x, x
+
+
+class Place:
+    def __init__(self, zs, xs):
+        self.zs, self.xs = zs, xs
+        self.segment = lax.axis_index("segment")
+        self.me = lax.axis_index("dp")
+        self.z, self.x = self.me // xs, self.me % xs
+
+    def at(self, z, x):
+        return (self.segment, z * self.xs + x)
+
+    def beside(self, j):
+        return lax.rem(self.x + j, self.xs)
+
+    def enter(self):
+        barrier = pltpu.get_barrier_semaphore()
+
+        def greet(z, x):
+            pl.semaphore_signal(barrier, inc=1, device_id=self.at(z, x), device_id_type=MESH)
+
+        for j in range(1, self.xs):
+            greet(self.z, self.beside(j))
+
+        @pl.when(self.z > 0)
+        def _():
+            greet(self.z - 1, self.x)
+
+        @pl.when(self.z < self.zs - 1)
+        def _():
+            greet(self.z + 1, self.x)
+
+        count = self.xs - 1 + jnp.where(self.z > 0, 1, 0) + jnp.where(self.z < self.zs - 1, 1, 0)
+        pl.semaphore_wait(barrier, count)
+
+    def copy(self, src, dst, send, recv, z, x):
+        return pltpu.make_async_remote_copy(
+            src_ref=src, dst_ref=dst, send_sem=send, recv_sem=recv,
+            device_id=self.at(z, x), device_id_type=MESH,
+        )
+
+
+def gather_kernel(
+    zs, xs, a_ref, b_ref, ga_ref, gb_ref,
+    own_sem, ax_send, ax_recv, bx_send, bx_recv, az_send, az_recv, bz_send, bz_recv,
+):
+    place = Place(zs, xs)
+    z, x = place.z, place.x
+    slots = a_ref.shape[0]
+    place.enter()
+
+    def own(l, which):
+        src, dst = (a_ref, ga_ref) if which == 0 else (b_ref, gb_ref)
+        return pltpu.make_async_copy(src.at[l], dst.at[l, z, x], own_sem.at[l, which])
+
+    def a_beside(l, j, from_x):
+        return place.copy(
+            a_ref.at[l], ga_ref.at[l, z, from_x], ax_send.at[l, j], ax_recv.at[l, j],
+            z, place.beside(j),
+        )
+
+    def b_beside(l, row, j, from_x):
+        return place.copy(
+            gb_ref.at[l, row, from_x], gb_ref.at[l, row, from_x],
+            bx_send.at[l, row, j], bx_recv.at[l, row, j], z, place.beside(j),
+        )
+
+    def line(which, l, way, step, row, to_z):
+        if which == 0:
+            ref, send, recv = ga_ref.at[l, row], az_send, az_recv
+        else:
+            ref, send, recv = gb_ref.at[l, row, x], bz_send, bz_recv
+        return place.copy(ref, ref, send.at[l, way, step], recv.at[l, way, step], to_z, x)
+
+    def sends(which, l, step, act):
+        @pl.when((z - step >= 0) & (z + 1 < zs))
+        def _():
+            act(line(which, l, 0, step, z - step, z + 1))
+
+        @pl.when((z + step < zs) & (z - 1 >= 0))
+        def _():
+            act(line(which, l, 1, step, z + step, z - 1))
+
+    def receives(which, l, step, then):
+        @pl.when(z - 1 - step >= 0)
+        def _():
+            line(which, l, 0, step, z - 1 - step, z).wait_recv()
+            then(z - 1 - step)
+
+        @pl.when(z + 1 + step < zs)
+        def _():
+            line(which, l, 1, step, z + 1 + step, z).wait_recv()
+            then(z + 1 + step)
+
+    def begin(c):
+        c.start()
+
+    def done(c):
+        c.wait_send()
+
+    def spread(l, row):
+        for j in range(1, xs):
+            b_beside(l, row, j, x).start()
+
+    for l in range(slots):
+        own(l, 0).start()
+        own(l, 1).start()
+        for j in range(1, xs):
+            a_beside(l, j, x).start()
+    for l in range(slots):
+        own(l, 1).wait()
+        sends(1, l, 0, begin)
+        spread(l, z)
+    for l in range(slots):
+        own(l, 0).wait()
+        for j in range(1, xs):
+            a_beside(l, j, lax.rem(x + xs - j, xs)).wait_recv()
+        sends(0, l, 0, begin)
+    for step in range(zs - 1):
+        for l in range(slots):
+            for which in (1, 0):
+                receives(which, l, step, partial(spread, l) if which == 1 else lambda row: None)
+                if step < zs - 2:
+                    sends(which, l, step + 1, begin)
+    for l in range(slots):
+        for j in range(1, xs):
+            a_beside(l, j, x).wait_send()
+            for row in range(zs):
+                b_beside(l, row, j, lax.rem(x + xs - j, xs)).wait_recv()
+                b_beside(l, row, j, x).wait_send()
+        for which in (0, 1):
+            for step in range(zs - 1):
+                sends(which, l, step, done)
+
+
+def gather_weights(a, b, dp):
+    zs, xs = grid_of(dp)
+    slots = a.shape[0]
+    dma = pltpu.SemaphoreType.DMA
+    ga, gb = pl.pallas_call(
+        partial(gather_kernel, zs, xs),
+        out_shape=tuple(
+            jax.ShapeDtypeStruct((slots, zs, xs) + w.shape[1:], w.dtype) for w in (a, b)
+        ),
+        in_specs=[pl.BlockSpec(memory_space=pl.ANY)] * 2,
+        out_specs=(pl.BlockSpec(memory_space=pl.ANY),) * 2,
+        scratch_shapes=[dma((slots, 2)), dma((slots, xs)), dma((slots, xs))]
+        + [dma((slots, zs, xs))] * 2
+        + [dma((slots, 2, zs))] * 4,
+        compiler_params=pltpu.CompilerParams(
+            collective_id=0, has_side_effects=True, vmem_limit_bytes=VMEM_BYTES
+        ),
+        name="gather_weights",
+    )(a, b)
+    return tuple(g.reshape((slots, -1) + g.shape[4:]) for g in (ga, gb))
+
+
+def scatter_kernel(
+    zs, xs, a_ref, b_ref, oa_ref, ob_ref,
+    a_line, b_line, a_sum, a_side, b_col, b_side,
+    ax_send, ax_recv, bx_send, bx_recv, az_send, az_recv, bz_send, bz_recv,
+):
+    place = Place(zs, xs)
+    z, x = place.z, place.x
+    slots, n = a_ref.shape[0], a_ref.shape[3]
+    f32, bf16 = jnp.float32, jnp.bfloat16
+    place.enter()
+
+    def each(count, body):
+        def step(i, carry):
+            body(i)
+            return carry
+
+        lax.fori_loop(0, count, step, 0)
+
+    def b_beside(l, j):
+        return place.copy(
+            b_ref.at[l, :, place.beside(j)], b_side.at[l, j], bx_send.at[l, j], bx_recv.at[l, j],
+            z, place.beside(j),
+        )
+
+    def a_beside(l, j):
+        return place.copy(
+            a_sum.at[l, place.beside(j)], a_side.at[l, j], ax_send.at[l, j], ax_recv.at[l, j],
+            z, place.beside(j),
+        )
+
+    def mine(which, l, row):
+        return a_ref.at[l, row] if which == 0 else b_col.at[l, row]
+
+    def line(which, l, way, step, src, to_z):
+        buf, send, recv = (
+            (a_line, az_send, az_recv) if which == 0 else (b_line, bz_send, bz_recv)
+        )
+        return place.copy(
+            src, buf.at[l, way, step], send.at[l, way, step], recv.at[l, way, step], to_z, x
+        )
+
+    def row_of(way, step):
+        return zs - 1 - step if way == 0 else step
+
+    def advance(which, l, way, step):
+        buf = (a_line if which == 0 else b_line).at[l, way, step]
+        row = row_of(way, step)
+        own = mine(which, l, row)
+        to_z = z + 1 if way == 0 else z - 1
+        first = z == 0 if way == 0 else z == zs - 1
+        beyond = z < row if way == 0 else z > row
+        ahead = z <= row if way == 0 else z >= row
+
+        @pl.when(jnp.logical_not(first) & ahead)
+        def _():
+            line(which, l, way, step, buf, z).wait_recv()
+
+        @pl.when(jnp.logical_not(first) & beyond)
+        def _():
+            def add(i):
+                at = (i // n, i % n) if which == 0 else (i,)
+                buf[at] = (buf[at].astype(f32) + own[at].astype(f32)).astype(bf16)
+
+            each(xs * n if which == 0 else n, add)
+            line(which, l, way, step, buf, to_z).start()
+
+        @pl.when(first & beyond)
+        def _():
+            line(which, l, way, step, own, to_z).start()
+
+    def finish_sends(which, l, way, step):
+        row = row_of(way, step)
+
+        @pl.when(z < row if way == 0 else z > row)
+        def _():
+            buf = (a_line if which == 0 else b_line).at[l, way, step]
+            line(which, l, way, step, buf, z + 1 if way == 0 else z - 1).wait_send()
+
+    for l in reversed(range(slots)):
+        for j in range(1, xs):
+            b_beside(l, j).start()
+    for l in reversed(range(slots)):
+        for way in (0, 1):
+            advance(0, l, way, 0)
+    for l in reversed(range(slots)):
+        for j in range(1, xs):
+            b_beside(l, j).wait_recv()
+
+        def column(i, l=l):
+            row, k = i // n, i % n
+            value = b_ref[l, row, x, k].astype(f32)
+            for j in range(1, xs):
+                value += b_side[l, j, row, k].astype(f32)
+            b_col[l, row, k] = value.astype(bf16)
+
+        each(zs * n, column)
+        for way in (0, 1):
+            advance(1, l, way, 0)
+    for step in range(1, zs - 1):
+        for l in reversed(range(slots)):
+            for which in (0, 1):
+                for way in (0, 1):
+                    advance(which, l, way, step)
+
+    for l in reversed(range(slots)):
+        right, left = jnp.clip(zs - 1 - z, 0, zs - 2), jnp.clip(z, 0, zs - 2)
+        has_right, has_left = z > 0, z < zs - 1
+
+        def start_sum(i, l=l):
+            p, k = i // n, i % n
+            a_sum[l, p, k] = a_ref[l, z, p, k]
+
+        def add_sum(way, at, i, l=l):
+            p, k = i // n, i % n
+            a_sum[l, p, k] = (
+                a_sum[l, p, k].astype(f32) + a_line[l, way, at, p, k].astype(f32)
+            ).astype(bf16)
+
+        each(xs * n, start_sum)
+        pl.when(has_right)(lambda: each(xs * n, partial(add_sum, 0, right)))
+        pl.when(has_left)(lambda: each(xs * n, partial(add_sum, 1, left)))
+        for j in range(1, xs):
+            a_beside(l, j).start()
+
+        def start_out(i, l=l):
+            ob_ref[l, i] = b_col[l, z, i].astype(f32)
+
+        def add_out(way, at, i, l=l):
+            ob_ref[l, i] += b_line[l, way, at, i].astype(f32)
+
+        each(n, start_out)
+        pl.when(has_right)(lambda: each(n, partial(add_out, 0, right)))
+        pl.when(has_left)(lambda: each(n, partial(add_out, 1, left)))
+    for l in reversed(range(slots)):
+        for j in range(1, xs):
+            a_beside(l, j).wait_recv()
+
+        def out(i, l=l):
+            value = a_sum[l, x, i].astype(f32)
+            for j in range(1, xs):
+                value += a_side[l, j, i].astype(f32)
+            oa_ref[l, i] = value
+
+        each(n, out)
+    for l in range(slots):
+        for j in range(1, xs):
+            a_beside(l, j).wait_send()
+            b_beside(l, j).wait_send()
+        for which in (0, 1):
+            for way in (0, 1):
+                for step in range(zs - 1):
+                    finish_sends(which, l, way, step)
+
+
+def scatter_grads(a, b, dp):
+    zs, xs = grid_of(dp)
+    slots, nb = a.shape[:2]
+    n = nb // dp
+    a, b = (g.reshape((slots, zs, xs, n) + g.shape[2:]) for g in (a, b))
+    ta, tb = a.shape[4:], b.shape[4:]
+    dma = pltpu.SemaphoreType.DMA
+    bf16 = jnp.bfloat16
+    vmem = pl.BlockSpec(memory_space=pltpu.VMEM)
+    return pl.pallas_call(
+        partial(scatter_kernel, zs, xs),
+        out_shape=tuple(
+            jax.ShapeDtypeStruct((slots, n) + t, jnp.float32) for t in (ta, tb)
+        ),
+        in_specs=[vmem, vmem],
+        out_specs=(vmem, vmem),
+        scratch_shapes=[
+            pltpu.VMEM((slots, 2, zs - 1, xs, n) + ta, bf16),
+            pltpu.VMEM((slots, 2, zs - 1, n) + tb, bf16),
+            pltpu.VMEM((slots, xs, n) + ta, bf16),
+            pltpu.VMEM((slots, xs, n) + ta, bf16),
+            pltpu.VMEM((slots, zs, n) + tb, bf16),
+            pltpu.VMEM((slots, xs, zs, n) + tb, bf16),
+        ]
+        + [dma((slots, xs))] * 4
+        + [dma((slots, 2, zs))] * 4,
+        compiler_params=pltpu.CompilerParams(
+            collective_id=1, has_side_effects=True, vmem_limit_bytes=VMEM_BYTES
+        ),
+        name="scatter_grads",
+    )(a, b)
+
+
 def whole(shape):
     return pl.BlockSpec(shape, lambda i: (0,) * len(shape))
 
 
 def forward_layer(x, w_in, w_out, gain):
     width, tokens = x.shape
-    nb, bi, bo = w_in.shape
+    nb, bi, bo = w_out.shape
+    wide = w_in.shape[1]
     group = min(GROUP, nb)
     steps = nb // group
     first = lambda i: (jnp.minimum(i, steps - 1), 0, 0)
@@ -158,7 +516,7 @@
         ),
         in_specs=[
             whole((width, tokens)),
-            pl.BlockSpec((group, bi, bo), first),
+            pl.BlockSpec((group, wide, bo), first),
             pl.BlockSpec((group, bi, bo), second),
             whole((width, tokens)),
         ],
@@ -178,26 +536,25 @@
 
 def backward_layer(x, g, w_in, w_out, gain, act, slope):
     width, tokens = x.shape
-    nb, bi, bo = w_in.shape
+    nb, bi, bo = w_out.shape
+    wide = w_in.shape[1]
     group = min(GROUP, nb)
     steps = nb // group
     first = lambda i: (jnp.minimum(i, steps - 1), 0, 0)
     first2 = lambda i: (jnp.minimum(i, steps - 1), 0)
     second = lambda i: (jnp.maximum(i - steps, 0), 0, 0)
-    weight = jax.ShapeDtypeStruct((nb, bi, bo), jnp.bfloat16)
     return pl.pallas_call(
         backward_kernel,
         grid=(2 * steps,),
         out_shape=(
             jax.ShapeDtypeStruct((width, tokens), jnp.bfloat16),
-            weight,
-            weight,
-            jax.ShapeDtypeStruct((width, 1), jnp.float32),
+            jax.ShapeDtypeStruct((nb, wide, bo), jnp.bfloat16),
+            jax.ShapeDtypeStruct((nb, bi, bo), jnp.bfloat16),
         ),
         in_specs=[
             whole((width, tokens)),
             whole((width, tokens)),
-            pl.BlockSpec((group, bi, bo), second),
+            pl.BlockSpec((group, wide, bo), second),
             pl.BlockSpec((group, bi, bo), first),
             whole((width, tokens)),
             pl.BlockSpec((group * bo, tokens), first2),
@@ -205,9 +562,8 @@
         ],
         out_specs=(
             whole((width, tokens)),
-            pl.BlockSpec((group, bi, bo), second),
+            pl.BlockSpec((group, wide, bo), second),
             pl.BlockSpec((group, bi, bo), first),
-            whole((width, 1)),
         ),
         scratch_shapes=[
             pltpu.VMEM((nb * bo, tokens), jnp.float32),
@@ -232,13 +588,20 @@
     micro, rows, width = inputs.shape
     tokens = micro * rows
     count_here = jnp.sum(jnp.where(jnp.arange(segment_count) == my_segment, counts, 0))
-    full_in = [lax.all_gather(w_in[0, l], "dp", axis=0, tiled=True) for l in range(slot_count)]
-    full_out = [lax.all_gather(w_out[0, l], "dp", axis=0, tiled=True) for l in range(slot_count)]
-    full_gain = lax.all_gather(gains[0], "dp", axis=1, tiled=True)
+    dp = lax.axis_size("dp")
+    own_nb, bi, bo = w_in.shape[2:]
+    nb = own_nb * dp
+    extra = 16
+    gain_rows = jnp.pad(
+        gains.reshape(slot_count, own_nb, 1, bi), ((0, 0), (0, 0), (0, extra - 1), (0, bo - bi))
+    )
+    full_in, full_out = gather_weights(
+        jnp.concatenate([w_in[0], gain_rows], axis=2), w_out[0], dp
+    )
     gain = [
-        jnp.broadcast_to(full_gain[l][:, None], (width, tokens)) for l in range(slot_count)
+        jnp.broadcast_to(full_in[l, :, bi, :bi].reshape(width, 1), (width, tokens))
+        for l in range(slot_count)
     ]
-    nb, bi, bo = full_in[0].shape
     first_x = to_columns(inputs)
     last_g = to_columns(cotangent)
 
@@ -287,9 +650,9 @@
                 g, *out[l] = lax.cond(l < count_here, live, lambda g, l=l: (g, *grads[l]), g)
         return g, tuple(tuple(o) for o in out)
 
-    zero_weight = jnp.zeros((nb, bi, bo), jnp.bfloat16)
-    zero_gain = jnp.zeros((width, 1), jnp.float32)
-    grads = tuple((zero_weight, zero_weight, zero_gain) for l in range(slot_count))
+    zero_in = jnp.zeros((nb, bi + extra, bo), jnp.bfloat16)
+    zero_out = jnp.zeros((nb, bi, bo), jnp.bfloat16)
+    grads = tuple((zero_in, zero_out) for l in range(slot_count))
     g = last_g
     down = g
     for k in reversed(range(segment_count)):
@@ -298,15 +661,14 @@
         if k > 0:
             g = lax.ppermute(g, "segment", [(k, k - 1)])
 
-    def scatter(a):
-        return lax.psum_scatter(
-            a.astype(jnp.bfloat16), "dp", scatter_dimension=0, tiled=True
-        ).astype(jnp.float32)
-
-    grad_in = jnp.stack([scatter(grads[l][0]) for l in range(slot_count)])[None]
-    grad_out = jnp.stack([scatter(grads[l][1]) for l in range(slot_count)])[None]
-    all_gain = jnp.stack([grads[l][2][:, 0] for l in range(slot_count)], axis=1)
-    grad_gain = scatter(all_gain).T[None]
+    sum_in, sum_out = scatter_grads(
+        jnp.stack([grads[l][0] for l in range(slot_count)]),
+        jnp.stack([grads[l][1] for l in range(slot_count)]),
+        dp,
+    )
+    grad_in = sum_in[None, :, :, :bi, :]
+    grad_out = sum_out[None]
+    grad_gain = sum_in[:, :, bi, :bi].reshape(1, slot_count, own_nb * bi)
     outputs = result.T.reshape(1, micro, rows, width)
     grads_kept = down.T.reshape(1, micro, rows, width)
     return outputs, grads_kept, grad_in, grad_out, grad_gain

time: 910 us -> 851 us (0.935)
  waiting for transfers between devices: 732 us -> 231 us
  Pallas kernels: 39 us -> 525 us
  blocking collectives: 25.1 us -> 0 us
  between operations: 14.2 us -> 1.09 us
    pallas_call x0 -> x2, Pallas kernels: none -> 440 us  [the longest x1 319 us: scatter_grads(): pl.pallas_call(partial(scatter_kernel, zs, xs), out_shape=tuple((jax.Shap...]
    reduce_scatter x4 -> x0, waiting for transfers between devices: 278 us -> none  [scatter(): lax.psum_scatter(a.astype(jnp.bfloat16), 'dp', scatter_dimension=0, tiled...]
    all_gather x4 -> x0, waiting for transfers between devices: 174 us -> none  [the longest x2 101 us: per_device(): lax.all_gather(w_out[0, l], 'dp', axis=0, tiled=True)]
    unnamed x10 -> x0, waiting for transfers between devices: 52.8 us -> none
    pallas_call x1 -> x2, Pallas kernels: 19.7 us -> 49.5 us  [backward_layer(): pl.pallas_call(backward_kernel, grid=(2 * steps,), out_shape=(jax.ShapeDt...]
    all_gather x1 -> x0, blocking collectives: 25.1 us -> none  [per_device(): full_gain = lax.all_gather(gains[0], 'dp', axis=1, tiled=True)]
    pallas_call x1 -> x2, Pallas kernels: 19.2 us -> 34.7 us  [forward_layer(): pl.pallas_call(forward_kernel, grid=(2 * steps,), out_shape=(jax.ShapeDty...]
    squeeze x0 -> x8, local copies, waits for them, and re-layouts: none -> 12.4 us  [the longest x4 7.86 us: live(): return forward_layer(x, full_in[l], full_out[l], gain[l])]
  transfers between devices with their start and end apart: 15 -> 6, of which waited for: 11 -> 2; matrix products, arithmetic and copies ran while one was open for 2% -> 1% of each run, Pallas kernels for 0% -> 0%
where the time goes in v2:
time: 851 us; the launch traced here: 842 us
  Pallas kernels  525 us (62%)
  waiting for transfers between devices  231 us (27%)
  local copies, waits for them, and re-layouts  50.2 us (6%)
  other arithmetic  15.8 us (2%)
  loops' own time  9.68 us (1%)
  starting transfers between devices  9.34 us (1%)
    pallas_call x1, Pallas kernels, scatter_grads(): pl.pallas_call(partial(scatter_kernel, zs, xs), out_shape=tuple((jax.Shap...  319 us
    ppermute x3, waiting for transfers between devices, per_device(): g = lax.ppermute(g, 'segment', [(k, k - 1)])  230 us
    pallas_call x1, Pallas kernels, gather_weights(): pl.pallas_call(partial(gather_kernel, zs, xs), out_shape=tuple((jax.Shape...  122 us
    pallas_call x2, Pallas kernels, backward_layer(): pl.pallas_call(backward_kernel, grid=(2 * steps,), out_shape=(jax.ShapeDt...  49.5 us
    pallas_call x2, Pallas kernels, forward_layer(): pl.pallas_call(forward_kernel, grid=(2 * steps,), out_shape=(jax.ShapeDty...  34.7 us
  transfers between devices with their start and end apart: 6, of which 2 were waited for; matrix products, arithmetic and copies ran while one was open for 1% of the time, Pallas kernels for 0%

profile of v2, /device:TPU:8, one launch (start us, length us, event | category | flops | bytes accessed | tf_op | source)
XLA Modules:
  0.0 842.0 jit_solution(13374474958447374680)
XLA Ops:
  4.9 121.5 %gather_weights.1 = (bf16[2,4,2,8,80,256]{5,4,3,2,1,0:T(8,128)(2,1)S(1)}, bf16[2,4,2,8,64,256]{5,4,3,2,1,0:T(8,128)(2,1)}) custom-call(bf16[2,8,80,256]{3,2,1,0:T(8,128)(2,1)S(1)} %fusion.1.a_ref, bf16[2,8,64,256]{3,2,1,0:T(8,128)(2,1)S(1)} %bitcast.90), custom_call_target="tpu_custom_call" | custom-call | tf_op jit(solution)/shard_map/gather_weights/pallas_call | solution.py:291
  126.5 2.3 copy-done.1
  130.4 45.3 %conditional.16 = (bf16[4096,128]{1,0:T(8,128)(2,1)}, bf16[4096,128]{1,0:T(8,128)(2,1)}, bf16[16384,128]{1,0:T(8,128)(2,1)}, bf16[16384,128]{1,0:T(8,128)(2,1)},...) conditional(s32[]{:T(128)} %convert_element_type.45, ...), branch_computations={%region_1.2_spmd, %region_2.5_spmd} | conditional | flops 2 | bytes 30408898 | solution.py:633
  133.0 2.2 slice_bitcast_fusion.3.w_out_ref
  135.2 1.9 slice_bitcast_fusion.2.w_in_ref
  137.2 16.7 %layer_forward.9 = (bf16[4096,128]{1,0:T(8,128)(2,1)}, bf16[16384,128]{1,0:T(8,128)(2,1)}, bf16[16384,128]{1,0:T(8,128)(2,1)}) custom-call(bf16[4096,128]{1,0:T(8,128)(2,1)S(1)} %copy.17.x_ref, bf16[64,80,256]{2,1,0:T(8,128)(2,1)S(1)} %slice_bitcast_fusion.2.w_in_ref, bf16[64,64,256]{2,1,0:T(8,128)(2,1)S(1)} %slice_bitcast_fusion.3.w_out_ref, ...), custom_call_target="tpu_custom_call" | custom-call | tf_op jit(solution)/shard_map/cond/branch_1_fun/layer_forward/pallas_call | solution.py:509
  153.9 21.8 %conditional = ((bf16[4096,128]{1,0:T(8,128)(2,1)}, bf16[16384,128]{1,0:T(8,128)(2,1)}, bf16[16384,128]{1,0:T(8,128)(2,1)})) conditional(s32[]{:T(128)} %convert_element_type.12, bf16[4096,128]{1,0:T(8,128)(2,1)} %get-tuple-element.837, (bf16[2,64,80,256]{3,2,1,0:T(8,128)(2,1)}, bf16[2,64,64,256]{3,2,1,0:T(8,128)(2,1)}, bf16[4096,128]{1,0:T(8,128)(2,1)}, ...), branch_computations={%region_3.3_spmd, %region_4.4_spmd} | conditional | bytes 10485796 | solution.py:618
  153.9 1.8 slice_bitcast_fusion.1.w_out_ref
  155.7 1.9 slice_bitcast_fusion.w_in_ref
  157.7 18.0 %layer_forward.8 = (bf16[4096,128]{1,0:T(8,128)(2,1)}, bf16[16384,128]{1,0:T(8,128)(2,1)}, bf16[16384,128]{1,0:T(8,128)(2,1)}) custom-call(bf16[4096,128]{1,0:T(8,128)(2,1)} %get-tuple-element.407.x_ref, bf16[64,80,256]{2,1,0:T(8,128)(2,1)S(1)} %slice_bitcast_fusion.w_in_ref, bf16[64,64,256]{2,1,0:T(8,128)(2,1)S(1)} %slice_bitcast_fusion.1.w_out_ref, ...), custom_call_target="tpu_custom_call" | custom-call | tf_op jit(solution)/shard_map/cond/branch_1_fun/cond/branch_1_fun/layer_forward/pallas_call | solution.py:509
  175.7 2.3 collective-permute-start
  182.9 2.3 conditional.18
  182.9 2.3 copy.31
  187.3 15.9 %conditional.20 = (bf16[4096,128]{1,0:T(8,128)(2,1)S(1)}, bf16[64,80,256]{2,1,0:T(8,128)(2,1)}, bf16[64,64,256]{2,1,0:T(8,128)(2,1)}, bf16[64,80,256]{2,1,0:T(8,128)(2,1)}, bf16[64,64,256]{2,1,0:T(8,128)(2,1)}) conditional(s32[]{:T(128)} %convert_element_type.42, (bf16[4096,128]{0,1:T(8,128)(2,1)}) %tuple.257, (s32[]{:T(128)}, ...), branch_computations={%region_17.18_spmd, %region_18.21_spmd} | conditional | flops 2 | bytes 52429004 | solution.py:659
  204.8 2.3 conditional.21
  204.8 2.3 copy.36
  208.7 2.3 conditional.22
  208.7 2.3 copy.38
  212.4 2.3 copy.18
  214.6 2.3 copy.24
  216.9 229.7 %collective-permute-done.5 = bf16[4096,128]{1,0:T(8,128)(2,1)} collective-permute-done((bf16[4096,128]{1,0:T(8,128)(2,1)}, bf16[4096,128]{1,0:T(8,128)(2,1)}, u32[]{:S(2)}, u32[]{:S(2)}) %collective-permute-start.5) | collective-permute-done | bytes 1048608 | tf_op jit(solution)/shard_map/ppermute | solution.py:662
  446.6 57.8 %conditional.23 = (bf16[4096,128]{1,0:T(8,128)(2,1)}, bf16[64,80,256]{2,1,0:T(8,128)(2,1)}, bf16[64,64,256]{2,1,0:T(8,128)(2,1)}, bf16[64,80,256]{2,1,0:T(8,128)(2,1)}, bf16[64,64,256]{2,1,0:T(8,128)(2,1)}) conditional(s32[]{:T(128)} %convert_element_type.45, (bf16[64,80,256]{2,1,0:T(8,128)(2,1)}, bf16[64,64,256]{2,1,0:T(8,128)(2,1)}, ...), branch_computations={%region_29.30_spmd, %region_30.33_spmd} | conditional | flops 2 | bytes 65011908 | solution.py:659
  447.1 28.8 %conditional.7 = ((bf16[4096,128]{1,0:T(8,128)(2,1)}, bf16[64,80,256]{2,1,0:T(8,128)(2,1)}, bf16[64,64,256]{2,1,0:T(8,128)(2,1)})) conditional(s32[]{:T(128)} %convert_element_type.37, (bf16[4096,128]{1,0:T(8,128)(2,1)}, bf16[64,80,256]{2,1,0:T(8,128)(2,1)}, bf16[64,64,256]{2,1,0:T(8,128)(2,1)}) %tuple.127, (bf16[2,64,80,256]{3,2,1,0:T(8,128)(2,1)}, ...), branch_computations={%region_31.31_spmd, %region_32.32_spmd} | conditional | bytes 32505892 | solution.py:650
  448.7 2.1 slice_bitcast_fusion.29.w_out_ref
  451.1 24.9 %layer_backward.14 = (bf16[4096,128]{1,0:T(8,128)(2,1)}, bf16[64,80,256]{2,1,0:T(8,128)(2,1)}, bf16[64,64,256]{2,1,0:T(8,128)(2,1)}) custom-call(bf16[4096,128]{1,0:T(8,128)(2,1)} %get-tuple-element.561.x_ref, bf16[4096,128]{1,0:T(8,128)(2,1)S(1)} %copy.205.g_ref, bf16[64,80,256]{2,1,0:T(8,128)(2,1)S(1)} %slice_bitcast_fusion.28.w_in_ref, ...), custom_call_target="tpu_custom_call" | custom-call | tf_op jit(solution)/shard_map/cond/branch_1_fun/cond/branch_1_fun/layer_backward/pallas_call | solution.py:546
  477.4 2.1 slice_bitcast_fusion.31.w_out_ref
  479.7 24.5 %layer_backward.15 = (bf16[4096,128]{1,0:T(8,128)(2,1)}, bf16[64,80,256]{2,1,0:T(8,128)(2,1)}, bf16[64,64,256]{2,1,0:T(8,128)(2,1)}) custom-call(bf16[4096,128]{1,0:T(8,128)(2,1)S(1)} %get-tuple-element.568.x_ref, bf16[4096,128]{1,0:T(8,128)(2,1)S(1)} %copy.206.g_ref, bf16[64,80,256]{2,1,0:T(8,128)(2,1)S(1)} %slice_bitcast_fusion.30.w_in_ref, ...), custom_call_target="tpu_custom_call" | custom-call | tf_op jit(solution)/shard_map/cond/branch_1_fun/layer_backward/pallas_call | solution.py:546
  504.4 4.6 pad_maximum_fusion.1.b_ref
  509.1 5.4 pad_maximum_fusion.a_ref
  514.4 318.9 %scatter_grads.1 = (f32[2,8,80,256]{3,2,1,0:T(8,128)S(1)}, f32[2,8,64,256]{3,2,1,0:T(8,128)S(1)}) custom-call(bf16[2,4,2,8,80,256]{5,4,3,2,1,0:T(8,128)(2,1)} %pad_maximum_fusion.a_ref, bf16[2,4,2,8,64,256]{5,4,3,2,1,0:T(8,128)(2,1)} %pad_maximum_fusion.1.b_ref), custom_call_target="tpu_custom_call" | custom-call | tf_op jit(solution)/shard_map/scatter_grads/pallas_call | solution.py:472
  835.1 2.3 copy.27
  837.4 3.3 select_select_fusion
  (59 shorter events, 36.2 us)
Async XLA Ops:
  0.6 129.8 %copy-start.19 = (bf16[2,64,4096]{2,1,0:T(8,128)(2,1)S(1)}, bf16[2,64,4096]{2,1,0:T(8,128)(2,1)}, u32[]{:S(2)}) copy-start(bf16[2,64,4096]{2,1,0:T(8,128)(2,1)} %param.38) | copy-start | bytes 3145732
  3.9 1.0 copy-start
  126.5 2.4 copy-start.1
  130.4 1.0 copy-start.21
  133.0 4.1 copy-start.12
  175.7 3.9 collective-permute-start
  181.3 1.7 copy-start.23
  181.3 1.7 collective-permute-start.1
  185.2 0.7 collective-permute-start.2
  203.1 1.6 copy-start.22
  203.1 1.6 collective-permute-start.3
  207.1 1.6 collective-permute-start.4
  211.0 235.6 %copy-start.13 = (bf16[4096,128]{1,0:T(8,128)(2,1)S(1)}, bf16[4096,128]{1,0:T(8,128)(2,1)}, u32[]{:S(2)}) copy-start(bf16[4096,128]{1,0:T(8,128)(2,1)} %get-tuple-element.672) | copy-start | bytes 3145732
  211.0 235.6 %collective-permute-start.5 = (bf16[4096,128]{1,0:T(8,128)(2,1)}, bf16[4096,128]{1,0:T(8,128)(2,1)}, u32[]{:S(2)}, u32[]{:S(2)}) collective-permute-start(bf16[4096,128]{1,0:T(8,128)(2,1)} %get-tuple-element.689), channel_id=1, source_target_pairs={{8,0},{9,1},{10,2},{11,3},{12,4},{13,5},{14,6},{15,7}} | collective-permute-start | bytes 3145736 | tf_op jit(solution)/shard_map/ppermute | solution.py:662
  447.4 3.5 copy-start.11
  476.0 3.5 copy-start.10
  833.3 4.1 copy-start.18
  833.4 4.0 copy-start.20
